TPU v7x, 256 devices: a whole 4x4x8 slice. The times are simulated.
256 devices in a mesh: outer: 4 (over z_hi, core), dp: 64 (over y, z_lo, x).
Axes of the slice: x: 4, y: 4, z: 8 (z_hi: 2, z_lo: 4; z = z_hi * 4 + z_lo), core: 2. Of those that a mesh axis runs over, the one named last changes fastest.
Arguments:
- gradients: bfloat16 [4, 64, 256, 128, 128], P('outer', 'dp'), may hold values from -6 to 6
- sign_flips: int32 [128, 128], replicated, may hold values from -1 to 1, as said below
Outputs:
- mean_code: float32 [256, 128, 128], P('dp', 'outer')
- gradient_sum: bfloat16 [256, 128, 128], replicated
Inputs may be any that keep to these rules, and one draw needn't show every extreme that they name: `sign_flips`: each entry is -1 or +1.
All inputs are finite; a program needn't handle non-finite values.
Results may differ from a plain program's by a relative error of at most 0.0029.
Values may be sent and summed in bfloat16 or wider, within the bound.
No kernel may reach another device: no remote copies, remote signals or barrier semaphores. Data moves between devices by JAX's collectives and lax.ppermute only.
A program may use at most 128 MiB of HBM per device.

v0:
```python
import jax
import jax.numpy as jnp
from jax import lax
from jax.sharding import PartitionSpec as P


def hadamard(length):
    index_row = jnp.arange(length, dtype=jnp.int32)[:, None]
    index_col = jnp.arange(length, dtype=jnp.int32)[None, :]
    common_bits = index_row & index_col
    parity = jnp.zeros((length, length), jnp.int32)
    for bit_pos in range(length.bit_length() - 1):
        parity = parity + (common_bits >> bit_pos & 1)
    return (1 - 2 * (parity % 2)).astype(jnp.float32)


def rotate(blocks_f, sign_f, hadamard_mat):
    length = hadamard_mat.shape[0]
    flipped = blocks_f * sign_f
    first_pass = jnp.einsum("bij,jk->bik", flipped, hadamard_mat, precision=lax.Precision.HIGHEST)
    return jnp.einsum(
        "ij,bjk->bik", hadamard_mat, first_pass, precision=lax.Precision.HIGHEST
    ) / float(length)


def quantize(rotated, maximum):
    return jnp.floor(rotated * (127.0 / maximum) + 0.5).astype(jnp.bfloat16)


def decode(code_total, sign_f, hadamard_mat, maximum):
    length = hadamard_mat.shape[0]
    first_pass = jnp.einsum(
        "bij,jk->bik", code_total, hadamard_mat, precision=lax.Precision.HIGHEST
    )
    second_pass = jnp.einsum(
        "ij,bjk->bik", hadamard_mat, first_pass, precision=lax.Precision.HIGHEST
    )
    return (second_pass * sign_f * (maximum / (127.0 * length))).astype(jnp.bfloat16)


def body(gradients, sign_flips):
    length = gradients.shape[-1]
    hadamard_mat = hadamard(length)
    sign_f = sign_flips.astype(jnp.float32)
    rotated = rotate(gradients[0, 0].astype(jnp.float32), sign_f, hadamard_mat)
    maximum = lax.pmax(jnp.max(jnp.abs(rotated)), ("outer", "dp"))
    code_vals = quantize(rotated, maximum)
    code_terms = code_vals.astype(jnp.float32)
    pod_share = lax.psum_scatter(code_terms, "dp", scatter_dimension=0, tiled=True)
    code_total = lax.psum(pod_share, "outer")
    workers = lax.axis_size("outer") * lax.axis_size("dp")
    mean_block = code_total / float(workers)
    row_count = length // lax.axis_size("outer")
    mean_rows = lax.dynamic_slice_in_dim(
        mean_block, lax.axis_index("outer") * row_count, row_count, 1
    )
    decoded_local = decode(code_total, sign_f, hadamard_mat, maximum)
    gradient_sum = lax.all_gather(decoded_local, "dp", axis=0, tiled=True)
    return (mean_rows, gradient_sum)


def solution(mesh):
    placed = (P("outer", "dp", None, None, None), P())
    return jax.shard_map(
        body, mesh=mesh, in_specs=placed, out_specs=(P("dp", "outer", None), P()), check_vma=False
    )
```

profile of v0, /device:TPU:2, one launch (start us, length us, event | category | flops | bytes accessed | tf_op | source)
XLA Modules:
  0.0 970.3 jit_solution(1639766023175889828)
XLA Ops:
  7.2 0.0 reduce-scatter.2.cloned.1.call-start
  7.2 0.8 convert_element_type.32
  8.1 20.3 %fusion = f32[256,128,128]{1,2,0:T(8,128)S(1)} fusion(bf16[1,1,256,128,128]{4,3,2,1,0:T(8,128)(2,1)} %param.2, f32[128,128]{1,0:T(8,128)S(1)} %convert_element_type.32), kind=kOutput, calls=%fused_computation.1 | convolution fusion | flops 6451412992 | bytes 25231360 | tf_op jit(solution)/shard_map/bij,jk->bik/dot_general | solution.py:20
  28.4 16.5 %abs_reduce_fusion = (f32[]{:T(128)}, f32[256,128,128]{2,1,0:T(8,128)}) fusion(f32[256,128,128]{1,2,0:T(8,128)S(1)} %fusion), kind=kOutput, calls=%fused_computation.4 | convolution fusion | flops 6455607296 | bytes 33554436 | tf_op jit(solution)/shard_map/ij,bjk->bik/dot_general | solution.py:21
  44.9 78.6 %pmax.7 = f32[]{:T(128)} all-reduce(f32[]{:T(128)} %get-tuple-element.6), channel_id=1, replica_groups=mesh['outer'=4,'dp'=64] {'outer','dp'}, use_global_device_ids=true, to_apply=%region_1.2 | all-reduce | flops 1 | bytes 8 | tf_op jit(solution)/shard_map/pmax | solution.py:46
  124.2 12.2 %convert_bitcast_fusion = f32[256,128,128]{1,2,0:T(8,128)} fusion(f32[256,128,128]{2,1,0:T(8,128)} %get-tuple-element.7, f32[]{:T(128)S(6)} %mul.46), kind=kLoop, calls=%fused_computation.2 | loop fusion | flops 20971520 | bytes 33554436 | tf_op jit(solution)/shard_map/convert_element_type | solution.py:48
  136.4 0.0 reduce-scatter.2.cloned.1.call-update
  136.4 0.0 all-reduce.2.cloned.1.call-start
  136.5 400.9 %reduce-scatter.2.cloned.1.call-done = f32[4,128,128]{1,2,0:T(8,128)} async-done(((f32[256,128,128]{1,2,0:T(8,128)}), f32[4,128,128]{1,2,0:T(8,128)}) %reduce-scatter.2.cloned.1.call-update) | async-done | bytes 262160 | tf_op jit(solution)/shard_map/reduce_scatter | solution.py:49
  537.4 0.0 all-reduce.2.cloned.1.call-update
  537.4 0.2 all-gather.2.cloned.1.call-start
  537.7 0.1 copy.7
  538.4 55.3 %all-reduce.2.cloned.1.call-done = f32[4,128,128]{1,2,0:T(8,128)} async-done(((f32[4,128,128]{1,2,0:T(8,128)}), f32[4,128,128]{1,2,0:T(8,128)}) %all-reduce.2.cloned.1.call-update) | async-done | bytes 262160 | tf_op jit(solution)/shard_map/psum | solution.py:50
  593.7 1.4 fusion.12
  595.2 0.4 fusion.5
  595.6 0.8 copy.8
  596.4 0.0 all-gather.2.cloned.1.call-update
  596.4 1.1 dynamic-slice_multiply_fusion
  597.5 0.7 copy.9
  598.2 355.0 %all-gather.2.cloned.1.call-done = bf16[256,128,128]{2,1,0:T(8,128)(2,1)} async-done(((bf16[4,128,128]{2,1,0:T(8,128)(2,1)}), bf16[256,128,128]{2,1,0:T(8,128)(2,1)}) %all-gather.2.cloned.1.call-update) | async-done | bytes 8388624 | tf_op jit(solution)/shard_map/all_gather | solution.py:58
  953.3 10.5 %copy.12 = bf16[256,128,128]{2,1,0:T(8,128)(2,1)} copy(bf16[256,128,128]{2,1,0:T(8,128)(2,1)} %all-gather.2.cloned.1.call-done) | data formatting | bytes 16777216
Async XLA Ops:
  7.2 530.3 %reduce-scatter.2.cloned.1.call-start = ((), (), s32[]{:S(2)}) async-start(), calls=%async_computation.1 | async-start | bytes 17039360 | tf_op jit(solution)/shard_map/reduce_scatter | solution.py:49
  136.4 457.3 %all-reduce.2.cloned.1.call-start = ((), (), s32[]{:S(2)}) async-start(), calls=%async_computation.2 | async-start | bytes 524288 | tf_op jit(solution)/shard_map/psum | solution.py:50
  537.4 415.8 %all-gather.2.cloned.1.call-start = ((), (), s32[]{:S(2)}) async-start(), calls=%async_computation.3 | async-start | bytes 8519680 | tf_op jit(solution)/shard_map/all_gather | solution.py:58
Sparse Core Ops, SparseCore 0:
  136.6 400.8 reduce-scatter.1
  540.1 53.6 all-reduce.1
  596.5 356.6 all-gather.1
where the time goes:
time: 971 us; the launch traced here: 970 us
  waiting for transfers between devices  811 us (84%)
  blocking collectives  78.6 us (8%)
  matrix products  38.7 us (4%)
  between operations  15.1 us (2%)
  other arithmetic  14.1 us (1%)
  local copies, waits for them, and re-layouts  12.1 us (1%)
    reduce_scatter x1, waiting for transfers between devices, body(): lax.psum_scatter(code_terms, 'dp', scatter_dimension=0, tiled=True)  401 us
    all_gather x1, waiting for transfers between devices, body(): gradient_sum = lax.all_gather(decoded_local, 'dp', axis=0, tiled=True)  355 us
    pmax x1, blocking collectives, body(): maximum = lax.pmax(jnp.max(jnp.abs(rotated)), ('outer', 'dp'))  78.6 us
    psum x1, waiting for transfers between devices, body(): code_total = lax.psum(pod_share, 'outer')  55.3 us
    dot_general x1, matrix products, rotate(): jnp.einsum('bij,jk->bik', flipped, hadamard_mat, precision=lax.Precision....  20.3 us
  transfers between devices with their start and end apart: 3, of which 3 were waited for; matrix products, arithmetic and copies ran while one was open for 0% of the time, Pallas kernels for 0%

commit v1 on v0

v1 whole, which is shorter than its diff:
```python
import functools

import jax
import jax.numpy as jnp
from jax import lax
from jax.experimental import pallas as pl
from jax.experimental.pallas import tpu as pltpu
from jax.sharding import PartitionSpec as P

AXES = ("outer", "dp")
NX, NY, NZ, NC = 4, 4, 8, 2
PASS = 128
HALF = PASS // 2
VMEM = 48 * 1024 * 1024


def coords(index):
    outer, dp = divmod(index, 64)
    return (outer // 2) * 4 + dp // 4 % 4, dp // 16, dp % 4, outer % 2


def linear(z, y, x, c):
    return ((z // 4) * 2 + c) * 64 + (y * 4 + z % 4) * 4 + x


def swap(array, z=0, y=0, x=0, c=0):
    pairs = []
    for index in range(256):
        at = coords(index)
        pairs.append((index, linear(at[0] ^ z, at[1] ^ y, at[2] ^ x, at[3] ^ c)))
    return lax.ppermute(array, AXES, pairs)


def hadamard(length):
    index_row = jnp.arange(length, dtype=jnp.int32)[:, None]
    index_col = jnp.arange(length, dtype=jnp.int32)[None, :]
    common_bits = index_row & index_col
    parity = jnp.zeros((length, length), jnp.int32)
    for bit_pos in range(length.bit_length() - 1):
        parity = parity + (common_bits >> bit_pos & 1)
    return (1 - 2 * (parity % 2)).astype(jnp.float32)


def split3(value):
    high = value.astype(jnp.bfloat16)
    rest = value - high.astype(jnp.float32)
    mid = rest.astype(jnp.bfloat16)
    low = (rest - mid.astype(jnp.float32)).astype(jnp.bfloat16)
    return high, mid, low


def dot(a, b):
    return jnp.dot(a, b, preferred_element_type=jnp.float32)


def params():
    return pltpu.CompilerParams(vmem_limit_bytes=VMEM)


def cost(flops, nbytes):
    return pl.CostEstimate(flops=flops, bytes_accessed=nbytes, transcendentals=0)


STEP = 8


def rotate_kernel(at_ref, x_ref, sign_ref, h_ref, out_ref, max_ref):
    h = h_ref[...]
    flipped = x_ref[...] * sign_ref[...][None]
    first = dot(flipped.reshape(STEP * PASS, PASS), h)
    high, mid, low = split3(first)
    peak = jnp.zeros((8, PASS), jnp.float32)
    for b in range(STEP):
        rows = slice(b * PASS, (b + 1) * PASS)
        turned = (dot(h, high[rows]) + (dot(h, mid[rows]) + dot(h, low[rows]))) * (1.0 / PASS)
        out_ref[b] = turned
        peak = jnp.maximum(peak, jnp.max(jnp.abs(turned).reshape(16, 8, PASS), axis=0))

    @pl.when(pl.program_id(0) == 0)
    def _():
        max_ref[...] = jnp.zeros_like(max_ref)

    max_ref[...] = jnp.maximum(max_ref[...], peak)


def rotate(blocks, at, sign, h):
    steps = 128 // STEP
    return pl.pallas_call(
        rotate_kernel,
        grid_spec=pltpu.PrefetchScalarGridSpec(
            num_scalar_prefetch=1,
            grid=(steps,),
            in_specs=[
                pl.BlockSpec((STEP, PASS, PASS), lambda i, at: (at[0] * steps + i, 0, 0)),
                pl.BlockSpec((PASS, PASS), lambda i, at: (0, 0)),
                pl.BlockSpec((PASS, PASS), lambda i, at: (0, 0)),
            ],
            out_specs=[
                pl.BlockSpec((STEP, PASS, PASS), lambda i, at: (i, 0, 0)),
                pl.BlockSpec((8, PASS), lambda i, at: (0, 0)),
            ],
        ),
        out_shape=[
            jax.ShapeDtypeStruct((128, PASS, PASS), jnp.float32),
            jax.ShapeDtypeStruct((8, PASS), jnp.float32),
        ],
        compiler_params=params(),
        cost_estimate=cost(8 * 128 * PASS**3, 12 << 20),
        name="rotate",
    )(at, blocks, sign, h)


def quantize_kernel(at_ref, max_ref, own_ref, mate_ref, *outs):
    scale = 127.0 / jnp.max(max_ref[...])
    my_y, my_x = at_ref[1], at_ref[2]
    for ky in range(NY):
        for kx in range(NX):
            b = (ky ^ my_y) * NX + (kx ^ my_x)
            code = jnp.floor(own_ref[b] * scale + 0.5) + jnp.floor(mate_ref[b] * scale + 0.5)
            code = code.astype(jnp.bfloat16)
            outs[kx][ky, 0] = code[:HALF]
            outs[NX + ky][kx, 0] = code[HALF:]


def quantize(maximum, own, mate, at):
    piece = jax.ShapeDtypeStruct((4, NZ, HALF, PASS), jnp.bfloat16)
    blocks = pl.BlockSpec((NY * NX, PASS, PASS), lambda i, at: (i ^ at[0], 0, 0))
    return pl.pallas_call(
        quantize_kernel,
        grid_spec=pltpu.PrefetchScalarGridSpec(
            num_scalar_prefetch=1,
            grid=(NZ,),
            in_specs=[pl.BlockSpec((8, PASS), lambda i, at: (0, 0)), blocks, blocks],
            out_specs=[pl.BlockSpec((4, 1, HALF, PASS), lambda i, at: (0, i, 0, 0))] * 8,
        ),
        out_shape=[piece] * 8,
        compiler_params=params(),
        cost_estimate=cost(1 << 24, 20 << 20),
        name="quantize",
    )(at, maximum, own, mate)


def add_first_kernel(*refs):
    total = refs[0][...].astype(jnp.float32)
    for ref in refs[1:4]:
        total = total + ref[...].astype(jnp.float32)
    total = total.astype(jnp.int32).astype(jnp.int16)
    for k in range(4):
        refs[4 + k][...] = total[k]


def add_first(pieces):
    return pl.pallas_call(
        add_first_kernel,
        grid=(2,),
        in_specs=[pl.BlockSpec((4, NZ // 2, HALF, PASS), lambda i: (0, i, 0, 0))] * 4,
        out_specs=[pl.BlockSpec((NZ // 2, HALF, PASS), lambda i: (i, 0, 0))] * 4,
        out_shape=[jax.ShapeDtypeStruct((NZ, HALF, PASS), jnp.int16)] * 4,
        compiler_params=params(),
        cost_estimate=cost(1 << 20, 5 << 19),
        name="add_first",
    )(*pieces)


def add_second_kernel(*refs):
    for half in range(2):
        terms = refs[4 * half : 4 * half + 4]
        total = terms[0][...].astype(jnp.int32)
        for ref in terms[1:]:
            total = total + ref[...].astype(jnp.int32)
        total = total.astype(jnp.int16)
        for k in range(NZ):
            refs[8 + k][half * HALF : (half + 1) * HALF] = total[k]


def add_second(top, bottom):
    return pl.pallas_call(
        add_second_kernel,
        out_shape=[jax.ShapeDtypeStruct((PASS, PASS), jnp.int16)] * NZ,
        compiler_params=params(),
        cost_estimate=cost(1 << 19, 5 << 18),
        name="add_second",
    )(*top, *bottom)


def decode_kernel(*refs):
    max_ref, sign_ref, h_ref = refs[:3]
    terms = refs[3 : 3 + NZ]
    total_ref, out_ref = refs[3 + NZ :]
    total = terms[0][...].astype(jnp.int32)
    for ref in terms[1:]:
        total = total + ref[...].astype(jnp.int32)
    total = total.astype(jnp.float32)
    total_ref[...] = total
    h = h_ref[...]
    high, mid, low = split3(total)
    first = dot(high, h) + (dot(mid, h) + dot(low, h))
    high, mid, low = split3(first)
    second = dot(h, high) + (dot(h, mid) + dot(h, low))
    unit = jnp.max(max_ref[...]) / (127.0 * PASS)
    out_ref[...] = (second * sign_ref[...].astype(jnp.float32) * unit).astype(jnp.bfloat16)


def decode(maximum, sign, h, terms):
    return pl.pallas_call(
        decode_kernel,
        out_shape=[
            jax.ShapeDtypeStruct((PASS, PASS), jnp.float32),
            jax.ShapeDtypeStruct((PASS, PASS), jnp.bfloat16),
        ],
        compiler_params=params(),
        cost_estimate=cost(12 * PASS**3, 1 << 19),
        name="decode",
    )(maximum, sign, h, *terms)


def assemble_kernel(at_ref, *refs):
    pieces, out_ref = refs[:8], refs[-1]
    my_y, my_x = at_ref[1], at_ref[2]
    for ky in range(NY):
        for kx in range(NX):
            b = (ky ^ my_y) * NX + (kx ^ my_x)
            out_ref[b, :HALF] = pieces[kx][ky, 0]
            out_ref[b, HALF:] = pieces[NX + ky][kx, 0]


def assemble(at, pieces, before=None):
    operands = [at, *pieces] + ([] if before is None else [before])
    return pl.pallas_call(
        assemble_kernel,
        grid_spec=pltpu.PrefetchScalarGridSpec(
            num_scalar_prefetch=1,
            grid=(NZ,),
            in_specs=[pl.BlockSpec((4, 1, HALF, PASS), lambda i, at: (0, i, 0, 0))] * 8
            + ([] if before is None else [pl.BlockSpec(memory_space=pl.ANY)]),
            out_specs=pl.BlockSpec((NY * NX, PASS, PASS), lambda i, at: (at[3] * NZ + (i ^ at[0]), 0, 0)),
        ),
        out_shape=jax.ShapeDtypeStruct((256, PASS, PASS), jnp.bfloat16),
        input_output_aliases={} if before is None else {9: 0},
        compiler_params=params(),
        cost_estimate=cost(1 << 10, 8 << 20),
        name="assemble",
    )(*operands)


def xor_order(array, index):
    array = jnp.where(index & 1 == 1, array[jnp.array([1, 0, 3, 2])], array)
    return jnp.where(index & 2 == 2, array[jnp.array([2, 3, 0, 1])], array)


def all_max(value):
    value = jnp.maximum(value, swap(value, c=1))
    for axis, size in (("x", NX), ("y", NY), ("z", NZ)):
        value = functools.reduce(jnp.maximum, [swap(value, **{axis: k}) for k in range(1, size)], value)
    return value


def mean_rows(total, outer, x):
    quarters = xor_order((total / 256.0).reshape(4, PASS // 4, PASS), x)
    got = []
    for r in range(4):
        pairs = []
        for index in range(256):
            z, y, px, c = coords(index)
            pairs.append((index, (px ^ r) * 64 + c * 32 + z * 4 + y))
        got.append(lax.ppermute(quarters[r], AXES, pairs))
    return xor_order(jnp.stack(got), outer)


def body(gradients, sign_flips):
    outer, dp = lax.axis_index("outer"), lax.axis_index("dp")
    z, y, x, c = (outer // 2) * 4 + dp // 4 % 4, dp // 16, dp % 4, outer % 2
    blocks = gradients[0, 0]
    h = hadamard(PASS).astype(jnp.bfloat16)
    sign = sign_flips.astype(jnp.bfloat16)

    def at(core):
        return jnp.stack([z, y, x, core]).astype(jnp.int32)

    mates = swap(lax.dynamic_slice_in_dim(blocks, (1 - c) * 128, 128, 0), c=1)
    own, own_max = rotate(blocks, jnp.stack([c]).astype(jnp.int32), sign, h)
    mate, mate_max = rotate(mates, jnp.zeros((1,), jnp.int32), sign, h)
    maximum = all_max(jnp.maximum(own_max, mate_max))

    pieces = quantize(maximum, own, mate, at(c))
    top, bottom = pieces[:4], pieces[4:]
    top = [top[0]] + [swap(top[k], x=k) for k in range(1, 4)]
    bottom = [bottom[0]] + [swap(bottom[k], y=k) for k in range(1, 4)]
    top, bottom = add_first(top), add_first(bottom)
    top = [top[0]] + [swap(top[k], y=k) for k in range(1, 4)]
    bottom = [bottom[0]] + [swap(bottom[k], x=k) for k in range(1, 4)]
    terms = add_second(top, bottom)
    terms = [terms[0]] + [swap(terms[k], z=k) for k in range(1, NZ)]
    total, decoded = decode(maximum, sign, h, terms)
    mean = mean_rows(total, outer, x)

    line = jnp.stack([decoded] + [swap(decoded, z=k) for k in range(1, NZ)])
    top, bottom = line[:, :HALF], line[:, HALF:]
    top = jnp.stack([top] + [swap(top, y=k) for k in range(1, 4)])
    bottom = jnp.stack([bottom] + [swap(bottom, x=k) for k in range(1, 4)])
    pieces = [top] + [swap(top, x=k) for k in range(1, 4)]
    pieces += [bottom] + [swap(bottom, y=k) for k in range(1, 4)]
    mates = [swap(piece, c=1) for piece in pieces]
    gradient_sum = assemble(at(c), pieces)
    gradient_sum = assemble(at(1 - c), mates, gradient_sum)
    return (mean, gradient_sum)


def solution(mesh):
    placed = (P("outer", "dp", None, None, None), P())
    return jax.shard_map(
        body, mesh=mesh, in_specs=placed, out_specs=(P("dp", "outer", None), P()), check_vma=False
    )
```

time: 971 us -> 275 us (0.28)
  the two profiles are of different devices: /device:TPU:2 before, /device:TPU:41 now
where the time goes in v1:
time: 275 us; the launch traced here: 270 us
  waiting for transfers between devices  107 us (39%)
  starting transfers between devices  104 us (38%)
  Pallas kernels  50.9 us (19%)
  local copies, waits for them, and re-layouts  5.19 us (2%)
    ppermute x61, starting transfers between devices, swap(): return lax.ppermute(array, AXES, pairs)  87.7 us
    ppermute x61, waiting for transfers between devices, swap(): return lax.ppermute(array, AXES, pairs)  57 us
    ppermute x4, waiting for transfers between devices, mean_rows(): got.append(lax.ppermute(quarters[r], AXES, pairs))  50 us
    pallas_call x2, Pallas kernels, rotate(): pl.pallas_call(rotate_kernel, grid_spec=pltpu.PrefetchScalarGridSpec(num_...  26.2 us
    ppermute x4, starting transfers between devices, mean_rows(): got.append(lax.ppermute(quarters[r], AXES, pairs))  16.6 us
    pallas_call x2, Pallas kernels, assemble(): pl.pallas_call(assemble_kernel, grid_spec=pltpu.PrefetchScalarGridSpec(nu...  13.3 us
    pallas_call x1, Pallas kernels, quantize(): pl.pallas_call(quantize_kernel, grid_spec=pltpu.PrefetchScalarGridSpec(nu...  9.76 us
  transfers between devices with their start and end apart: 65, of which 21 were waited for; matrix products, arithmetic and copies ran while one was open for 1% of the time, Pallas kernels for 8%

profile of v1, /device:TPU:41, one launch (start us, length us, event | category | flops | bytes accessed | tf_op | source)
XLA Modules:
  0.0 269.7 jit_solution(4195621887702527961)
XLA Ops:
  0.7 2.8 %dynamic-slice_bitcast_fusion = bf16[128,128,128]{2,1,0:T(8,128)(2,1)S(1)} fusion(bf16[1,1,256,128,128]{4,3,2,1,0:T(8,128)(2,1)} %param.6, s32[]{:T(128)S(6)} %select_n.83), kind=kLoop, calls=%fused_computation.4 | loop fusion | bytes 8388612 | tf_op jit(solution)/shard_map/dynamic_slice | solution.py:280
  4.3 14.8 %rotate.2 = (f32[128,128,128]{2,1,0:T(8,128)}, f32[8,128]{1,0:T(8,128)S(1)}) custom-call(s32[1]{0:T(128)} %bitcast.at_ref, bf16[256,128,128]{2,1,0:T(8,128)(2,1)} %bitcast.47, bf16[128,128]{1,0:T(8,128)(2,1)S(1)} %convert_element_type.17.sign_ref.refs_1_, bf16[128,128]{1,0:T(8,128)(2,1)S(1)} %fusion.4.h_ref.refs_2_), custom_call_target="tpu_custom_call" | custom-call | flops 2147483648 | bytes 12582912 | tf_op jit(solution)/shard_map/rotate/pallas_call | solution.py:88
  19.1 11.4 %rotate.3 = (f32[128,128,128]{2,1,0:T(8,128)}, f32[8,128]{1,0:T(8,128)S(1)}) custom-call(s32[1]{0:T(128)} %constant.94.clone.1.at_ref, bf16[128,128,128]{2,1,0:T(8,128)(2,1)S(1)} %collective-permute-done.x_ref, bf16[128,128]{1,0:T(8,128)(2,1)S(1)} %convert_element_type.17.sign_ref.refs_1_, bf16[128,128]{1,0:T(8,128)(2,1)S(1)} %fusion.4.h_ref.refs_2_), custom_call_target="tpu_custom_call" | custom-call | flops 2147483648 | bytes 12582912 | tf_op jit(solution)/shard_map/rotate/pallas_call | solution.py:88
  32.9 2.4 collective-permute-start.3
  36.8 2.2 collective-permute-done.4
  39.2 2.3 collective-permute-start.6
  41.6 1.5 collective-permute-done.6
  44.1 1.6 collective-permute-start.10
  45.7 5.1 %collective-permute-start.11 = (f32[8,128]{1,0:T(8,128)S(1)}, f32[8,128]{1,0:T(8,128)S(1)}, u32[]{:S(2)}, u32[]{:S(2)}) collective-permute-start(f32[8,128]{1,0:T(8,128)S(1)} %maximum_maximum_fusion.1), channel_id=1, source_target_pairs={{0,128},{1,129},{2,130},{3,131},{4,132},{5,133},{6,134},{7,135},{8... | collective-permute-start | bytes 12296 | tf_op jit(solution)/shard_map/ppermute | solution.py:31
  50.9 1.6 collective-permute-start.12
  52.6 2.4 collective-permute-start.13
  56.6 1.6 collective-permute-start.9
  58.3 2.1 collective-permute-done.14
  60.5 9.8 %quantize.1 = (bf16[4,8,64,128]{3,2,1,0:T(8,128)(2,1)S(1)}, bf16[4,8,64,128]{3,2,1,0:T(8,128)(2,1)S(1)}, bf16[4,8,64,128]{3,2,1,0:T(8,128)(2,1)S(1)}, bf16[4,8,6...) custom-call(s32[4]{0:T(128)S(1)} %pad_add_fusion.at_ref, ...), custom_call_target="tpu_custom_call" | custom-call | flops 16777216 | bytes 20971520 | tf_op jit(solution)/shard_map/quantize/pallas_call | solution.py:128
  70.3 3.0 %collective-permute-start.21 = (bf16[4,8,64,128]{3,2,1,0:T(8,128)(2,1)S(1)}, bf16[4,8,64,128]{3,2,1,0:T(8,128)(2,1)S(1)}, u32[]{:S(2)}, u32[]{:S(2)}) collective-permute-start(bf16[4,8,64,128]{3,2,1,0:T(8,128)(2,1)S(1)} %get-tuple-element.45), channel_id=1, source_target_pairs={{0,16},{1,17},{2,18},{3,19},{4,20},{5,21},{6,22},{7,23},{8,24},{9,... | collective-permute-start | bytes 1572872 | tf_op jit(solution)/shard_map/ppermute | solution.py:31
  74.8 1.9 collective-permute-start.16
  76.8 3.1 %collective-permute-done.21.refs_1_ = bf16[4,8,64,128]{3,2,1,0:T(8,128)(2,1)S(1)} collective-permute-done((bf16[4,8,64,128]{3,2,1,0:T(8,128)(2,1)S(1)}, bf16[4,8,64,128]{3,2,1,0:T(8,128)(2,1)S(1)}, u32[]{:S(2)}, u32[]{:S(2)}) %collective-permute-start.21) | collective-permute-done | bytes 524320 | tf_op jit(solution)/shard_map/ppermute | solution.py:31
  81.3 8.9 %collective-permute-done.22.refs_2_ = bf16[4,8,64,128]{3,2,1,0:T(8,128)(2,1)S(1)} collective-permute-done((bf16[4,8,64,128]{3,2,1,0:T(8,128)(2,1)S(1)}, bf16[4,8,64,128]{3,2,1,0:T(8,128)(2,1)S(1)}, u32[]{:S(2)}, u32[]{:S(2)}) %collective-permute-start.22) | collective-permute-done | bytes 524320 | tf_op jit(solution)/shard_map/ppermute | solution.py:31
  90.9 2.6 collective-permute-start.25
  95.3 2.1 collective-permute-start.18
  97.4 1.5 collective-permute-start.19
  100.5 6.9 %collective-permute-done.26.refs_7_ = s16[8,64,128]{2,1,0:T(8,128)(2,1)S(1)} collective-permute-done((s16[8,64,128]{2,1,0:T(8,128)(2,1)S(1)}, s16[8,64,128]{2,1,0:T(8,128)(2,1)S(1)}, u32[]{:S(2)}, u32[]{:S(2)}) %collective-permute-start.26) | collective-permute-done | bytes 131104 | tf_op jit(solution)/shard_map/ppermute | solution.py:31
  110.4 3.2 %collective-permute-start.30 = (s16[128,128]{1,0:T(8,128)(2,1)S(1)}, s16[128,128]{1,0:T(8,128)(2,1)S(1)}, u32[]{:S(2)}, u32[]{:S(2)}) collective-permute-start(s16[128,128]{1,0:T(8,128)(2,1)S(1)} %get-tuple-element.56), channel_id=1, source_target_pairs={{0,128},{1,129},{2,130},{3,131},{4,132},{5,133},{6,134},{7,135},{8... | collective-permute-start | bytes 98312 | tf_op jit(solution)/shard_map/ppermute | solution.py:31
  113.6 2.6 collective-permute-start.31
  117.6 1.7 collective-permute-start.33
  119.3 2.0 collective-permute-done.32.refs_9_
  121.3 2.0 collective-permute-done.33.refs_10_
  123.9 1.9 collective-permute-start.39
  126.5 2.2 collective-permute-start.41
  128.7 3.0 %collective-permute-start.42 = (bf16[128,128]{1,0:T(8,128)(2,1)S(1)}, bf16[128,128]{1,0:T(8,128)(2,1)S(1)}, u32[]{:S(2)}, u32[]{:S(2)}) collective-permute-start(bf16[128,128]{1,0:T(8,128)(2,1)S(1)} %get-tuple-element.61), channel_id=1, source_target_pairs={{0,132},{1,133},{2,134},{3,135},{4,128},{5,129},{6,130},{7,131},{8... | collective-permute-start | bytes 98312 | tf_op jit(solution)/shard_map/ppermute | solution.py:31
  131.7 10.7 %collective-permute-start.43 = (bf16[128,128]{1,0:T(8,128)(2,1)S(1)}, bf16[128,128]{1,0:T(8,128)(2,1)S(1)}, u32[]{:S(2)}, u32[]{:S(2)}) collective-permute-start(bf16[128,128]{1,0:T(8,128)(2,1)S(1)} %get-tuple-element.61), channel_id=1, source_target_pairs={{0,136},{1,137},{2,138},{3,139},{4,140},{5,141},{6,142},{7,143},{8... | collective-permute-start | bytes 98312 | tf_op jit(solution)/shard_map/ppermute | solution.py:31
  142.5 2.8 %collective-permute-start.44 = (bf16[128,128]{1,0:T(8,128)(2,1)S(1)}, bf16[128,128]{1,0:T(8,128)(2,1)S(1)}, u32[]{:S(2)}, u32[]{:S(2)}) collective-permute-start(bf16[128,128]{1,0:T(8,128)(2,1)S(1)} %get-tuple-element.61), channel_id=1, source_target_pairs={{0,140},{1,141},{2,142},{3,143},{4,136},{5,137},{6,138},{7,139},{8... | collective-permute-start | bytes 98312 | tf_op jit(solution)/shard_map/ppermute | solution.py:31
  146.7 1.7 collective-permute-done.44
  148.7 3.1 %collective-permute-start.56 = (bf16[8,64,128]{2,1,0:T(8,128)(2,1)S(1)}, bf16[8,64,128]{2,1,0:T(8,128)(2,1)S(1)}, u32[]{:S(2)}, u32[]{:S(2)}) collective-permute-start(bf16[8,64,128]{2,1,0:T(8,128)(2,1)S(1)} %get-tuple-element.66), channel_id=1, source_target_pairs={{0,2},{1,3},{2,0},{3,1},{4,6},{5,7},{6,4},{7,5},{8,10},{9,11},{10,... | collective-permute-start | bytes 393224 | tf_op jit(solution)/shard_map/ppermute | solution.py:31
  152.6 1.5 collective-permute-start.45
  156.9 1.8 collective-permute-start.59
  160.8 1.7 collective-permute-start.35
  162.5 26.9 %collective-permute-done.35 = f32[32,128]{1,0:T(8,128)S(1)} collective-permute-done((f32[32,128]{1,0:T(8,128)S(1)}, f32[32,128]{1,0:T(8,128)S(1)}, u32[]{:S(2)}, u32[]{:S(2)}) %collective-permute-start.35) | collective-permute-done | bytes 16416 | tf_op jit(solution)/shard_map/ppermute | solution.py:266
  189.4 9.1 %collective-permute-start.36 = (f32[32,128]{1,0:T(8,128)S(1)}, f32[32,128]{1,0:T(8,128)S(1)}, u32[]{:S(2)}, u32[]{:S(2)}) collective-permute-start(f32[32,128]{1,0:T(8,128)S(1)} %get-tuple-element.70), channel_id=1, source_target_pairs={{0,128},{1,192},{2,0},{3,64},{4,132},{5,196},{6,4},{7,68},{8,136},... | collective-permute-start | bytes 49160 | tf_op jit(solution)/shard_map/ppermute | solution.py:266
  199.8 3.1 %collective-permute-start.37 = (f32[32,128]{1,0:T(8,128)S(1)}, f32[32,128]{1,0:T(8,128)S(1)}, u32[]{:S(2)}, u32[]{:S(2)}) collective-permute-start(f32[32,128]{1,0:T(8,128)S(1)} %get-tuple-element.69), channel_id=1, source_target_pairs={{0,192},{1,128},{2,64},{3,0},{4,196},{5,132},{6,68},{7,4},{8,200},... | collective-permute-start | bytes 49160 | tf_op jit(solution)/shard_map/ppermute | solution.py:266
  202.9 13.8 %collective-permute-done.37 = f32[32,128]{1,0:T(8,128)S(1)} collective-permute-done((f32[32,128]{1,0:T(8,128)S(1)}, f32[32,128]{1,0:T(8,128)S(1)}, u32[]{:S(2)}, u32[]{:S(2)}) %collective-permute-start.37) | collective-permute-done | bytes 16416 | tf_op jit(solution)/shard_map/ppermute | solution.py:266
  216.7 2.8 %collective-permute-start.34 = (f32[32,128]{1,0:T(8,128)S(1)}, f32[32,128]{1,0:T(8,128)S(1)}, u32[]{:S(2)}, u32[]{:S(2)}) collective-permute-start(f32[32,128]{1,0:T(8,128)S(1)} %get-tuple-element.68), channel_id=1, source_target_pairs={{0,0},{1,64},{2,128},{3,192},{4,4},{5,68},{6,132},{7,196},{8,8},{9... | collective-permute-start | bytes 49160 | tf_op jit(solution)/shard_map/ppermute | solution.py:266
  219.4 8.0 %collective-permute-done.34 = f32[32,128]{1,0:T(8,128)S(1)} collective-permute-done((f32[32,128]{1,0:T(8,128)S(1)}, f32[32,128]{1,0:T(8,128)S(1)}, u32[]{:S(2)}, u32[]{:S(2)}) %collective-permute-start.34) | collective-permute-done | bytes 16416 | tf_op jit(solution)/shard_map/ppermute | solution.py:266
  228.8 4.7 %collective-permute-start.58 = (bf16[4,8,64,128]{3,2,1,0:T(8,128)(2,1)S(1)}, bf16[4,8,64,128]{3,2,1,0:T(8,128)(2,1)}, u32[]{:S(2)}, u32[]{:S(2)}) collective-permute-start(bf16[4,8,64,128]{3,2,1,0:T(8,128)(2,1)S(1)} %pad_maximum_fusion.1.refs_4_), channel_id=1, source_target_pairs={{0,64},{1,65},{2,66},{3,67},{4,68},{5,69},{6,70},{7,71},{8,72},{9,... | collective-permute-start | bytes 1572872 | tf_op jit(solution)/shard_map/ppermute | solution.py:31
  234.0 8.0 %collective-permute-done.51.refs_2_ = bf16[4,8,64,128]{3,2,1,0:T(8,128)(2,1)} collective-permute-done((bf16[4,8,64,128]{3,2,1,0:T(8,128)(2,1)S(1)}, bf16[4,8,64,128]{3,2,1,0:T(8,128)(2,1)}, u32[]{:S(2)}, u32[]{:S(2)}) %collective-permute-start.51) | collective-permute-done | bytes 524320 | tf_op jit(solution)/shard_map/ppermute | solution.py:31
  241.9 11.3 %collective-permute-done.53.refs_3_ = bf16[4,8,64,128]{3,2,1,0:T(8,128)(2,1)} collective-permute-done((bf16[4,8,64,128]{3,2,1,0:T(8,128)(2,1)S(1)}, bf16[4,8,64,128]{3,2,1,0:T(8,128)(2,1)}, u32[]{:S(2)}, u32[]{:S(2)}) %collective-permute-start.53) | collective-permute-done | bytes 524320 | tf_op jit(solution)/shard_map/ppermute | solution.py:31
  256.2 6.3 %assemble.2.refs_8_ = bf16[256,128,128]{2,1,0:T(8,128)(2,1)} custom-call(s32[4]{0:T(128)S(1)} %pad_add_fusion.at_ref, bf16[4,8,64,128]{3,2,1,0:T(8,128)(2,1)S(1)} %pad_maximum_fusion.refs_0_, bf16[4,8,64,128]{3,2,1,0:T(8,128)(2,1)S(1)} %collective-permute-done.49.refs_1_, bf16[4,8,64,128]{3,2,1,0:T(8,128)(2,1)} %collective-permute-done.51.refs_2_, ...), custom_call_target="tpu_custom_call" | custom-call | flops 1024 | bytes 8388608 | tf_op jit(solution)/shard_map/assemble/pallas_call | solution.py:229
  262.5 7.1 %assemble.3 = bf16[256,128,128]{2,1,0:T(8,128)(2,1)} custom-call(s32[4]{0:T(128)S(1)} %get-tuple-element.62.at_ref, bf16[4,8,64,128]{3,2,1,0:T(8,128)(2,1)} %collective-permute-done.48.refs_0_, bf16[4,8,64,128]{3,2,1,0:T(8,128)(2,1)} %collective-permute-done.50.refs_1_, ...), custom_call_target="tpu_custom_call", output_to_operand_aliasing={{}: (9, {})} | custom-call | flops 1024 | bytes 8388608 | tf_op jit(solution)/shard_map/assemble/pallas_call | solution.py:229
  (130 shorter events, 33.9 us)
Async XLA Ops:
  3.4 15.7 %collective-permute-start = (bf16[128,128,128]{2,1,0:T(8,128)(2,1)S(1)}, bf16[128,128,128]{2,1,0:T(8,128)(2,1)S(1)}, u32[]{:S(2)}, u32[]{:S(2)}) collective-permute-start(bf16[128,128,128]{2,1,0:T(8,128)(2,1)S(1)} %dynamic-slice_bitcast_fusion), channel_id=1, source_target_pairs={{0,64},{1,65},{2,66},{3,67},{4,68},{5,69},{6,70},{7,71},{8,72},{9,... | collective-permute-start | bytes 12582920 | tf_op jit(solution)/shard_map/ppermute | solution.py:31
  44.1 12.2 %collective-permute-start.10 = (f32[8,128]{1,0:T(8,128)S(1)}, f32[8,128]{1,0:T(8,128)S(1)}, u32[]{:S(2)}, u32[]{:S(2)}) collective-permute-start(f32[8,128]{1,0:T(8,128)S(1)} %maximum_maximum_fusion.1), channel_id=1, source_target_pairs={{0,12},{1,13},{2,14},{3,15},{4,8},{5,9},{6,10},{7,11},{8,4},{9,5},... | collective-permute-start | bytes 12296 | tf_op jit(solution)/shard_map/ppermute | solution.py:31
  45.7 10.9 %collective-permute-start.11 = (f32[8,128]{1,0:T(8,128)S(1)}, f32[8,128]{1,0:T(8,128)S(1)}, u32[]{:S(2)}, u32[]{:S(2)}) collective-permute-start(f32[8,128]{1,0:T(8,128)S(1)} %maximum_maximum_fusion.1), channel_id=1, source_target_pairs={{0,128},{1,129},{2,130},{3,131},{4,132},{5,133},{6,134},{7,135},{8... | collective-permute-start | bytes 12296 | tf_op jit(solution)/shard_map/ppermute | solution.py:31
  50.9 7.4 %collective-permute-start.12 = (f32[8,128]{1,0:T(8,128)S(1)}, f32[8,128]{1,0:T(8,128)S(1)}, u32[]{:S(2)}, u32[]{:S(2)}) collective-permute-start(f32[8,128]{1,0:T(8,128)S(1)} %maximum_maximum_fusion.1), channel_id=1, source_target_pairs={{0,132},{1,133},{2,134},{3,135},{4,128},{5,129},{6,130},{7,131},{8... | collective-permute-start | bytes 12296 | tf_op jit(solution)/shard_map/ppermute | solution.py:31
  70.3 9.6 %collective-permute-start.21 = (bf16[4,8,64,128]{3,2,1,0:T(8,128)(2,1)S(1)}, bf16[4,8,64,128]{3,2,1,0:T(8,128)(2,1)S(1)}, u32[]{:S(2)}, u32[]{:S(2)}) collective-permute-start(bf16[4,8,64,128]{3,2,1,0:T(8,128)(2,1)S(1)} %get-tuple-element.45), channel_id=1, source_target_pairs={{0,16},{1,17},{2,18},{3,19},{4,20},{5,21},{6,22},{7,23},{8,24},{9,... | collective-permute-start | bytes 1572872 | tf_op jit(solution)/shard_map/ppermute | solution.py:31
  73.3 16.9 %collective-permute-start.22 = (bf16[4,8,64,128]{3,2,1,0:T(8,128)(2,1)S(1)}, bf16[4,8,64,128]{3,2,1,0:T(8,128)(2,1)S(1)}, u32[]{:S(2)}, u32[]{:S(2)}) collective-permute-start(bf16[4,8,64,128]{3,2,1,0:T(8,128)(2,1)S(1)} %get-tuple-element.46), channel_id=1, source_target_pairs={{0,32},{1,33},{2,34},{3,35},{4,36},{5,37},{6,38},{7,39},{8,40},{9,... | collective-permute-start | bytes 1572872 | tf_op jit(solution)/shard_map/ppermute | solution.py:31
  73.3 16.9 %collective-permute-start.23 = (bf16[4,8,64,128]{3,2,1,0:T(8,128)(2,1)S(1)}, bf16[4,8,64,128]{3,2,1,0:T(8,128)(2,1)S(1)}, u32[]{:S(2)}, u32[]{:S(2)}) collective-permute-start(bf16[4,8,64,128]{3,2,1,0:T(8,128)(2,1)S(1)} %get-tuple-element.47), channel_id=1, source_target_pairs={{0,48},{1,49},{2,50},{3,51},{4,52},{5,53},{6,54},{7,55},{8,56},{9,... | collective-permute-start | bytes 1572872 | tf_op jit(solution)/shard_map/ppermute | solution.py:31
  74.6 19.0 %collective-permute-start.15 = (bf16[4,8,64,128]{3,2,1,0:T(8,128)(2,1)S(1)}, bf16[4,8,64,128]{3,2,1,0:T(8,128)(2,1)S(1)}, u32[]{:S(2)}, u32[]{:S(2)}) collective-permute-start(bf16[4,8,64,128]{3,2,1,0:T(8,128)(2,1)S(1)} %get-tuple-element.37), channel_id=1, source_target_pairs={{0,1},{1,0},{2,3},{3,2},{4,5},{5,4},{6,7},{7,6},{8,9},{9,8},{10,11... | collective-permute-start | bytes 1572872 | tf_op jit(solution)/shard_map/ppermute | solution.py:31
  74.8 19.9 %collective-permute-start.16 = (bf16[4,8,64,128]{3,2,1,0:T(8,128)(2,1)S(1)}, bf16[4,8,64,128]{3,2,1,0:T(8,128)(2,1)S(1)}, u32[]{:S(2)}, u32[]{:S(2)}) collective-permute-start(bf16[4,8,64,128]{3,2,1,0:T(8,128)(2,1)S(1)} %get-tuple-element.38), channel_id=1, source_target_pairs={{0,2},{1,3},{2,0},{3,1},{4,6},{5,7},{6,4},{7,5},{8,10},{9,11},{10,... | collective-permute-start | bytes 1572872 | tf_op jit(solution)/shard_map/ppermute | solution.py:31
  79.9 14.8 %collective-permute-start.17 = (bf16[4,8,64,128]{3,2,1,0:T(8,128)(2,1)S(1)}, bf16[4,8,64,128]{3,2,1,0:T(8,128)(2,1)S(1)}, u32[]{:S(2)}, u32[]{:S(2)}) collective-permute-start(bf16[4,8,64,128]{3,2,1,0:T(8,128)(2,1)S(1)} %get-tuple-element.39), channel_id=1, source_target_pairs={{0,3},{1,2},{2,1},{3,0},{4,7},{5,6},{6,5},{7,4},{8,11},{9,10},{10,... | collective-permute-start | bytes 1572872 | tf_op jit(solution)/shard_map/ppermute | solution.py:31
  90.7 8.1 %collective-permute-start.24 = (s16[8,64,128]{2,1,0:T(8,128)(2,1)S(1)}, s16[8,64,128]{2,1,0:T(8,128)(2,1)S(1)}, u32[]{:S(2)}, u32[]{:S(2)}) collective-permute-start(s16[8,64,128]{2,1,0:T(8,128)(2,1)S(1)} %get-tuple-element.49), channel_id=1, source_target_pairs={{0,1},{1,0},{2,3},{3,2},{4,5},{5,4},{6,7},{7,6},{8,9},{9,8},{10,11... | collective-permute-start | bytes 393224 | tf_op jit(solution)/shard_map/ppermute | solution.py:31
  90.9 9.6 %collective-permute-start.25 = (s16[8,64,128]{2,1,0:T(8,128)(2,1)S(1)}, s16[8,64,128]{2,1,0:T(8,128)(2,1)S(1)}, u32[]{:S(2)}, u32[]{:S(2)}) collective-permute-start(s16[8,64,128]{2,1,0:T(8,128)(2,1)S(1)} %get-tuple-element.50), channel_id=1, source_target_pairs={{0,2},{1,3},{2,0},{3,1},{4,6},{5,7},{6,4},{7,5},{8,10},{9,11},{10,... | collective-permute-start | bytes 393224 | tf_op jit(solution)/shard_map/ppermute | solution.py:31
  93.6 13.9 %collective-permute-start.26 = (s16[8,64,128]{2,1,0:T(8,128)(2,1)S(1)}, s16[8,64,128]{2,1,0:T(8,128)(2,1)S(1)}, u32[]{:S(2)}, u32[]{:S(2)}) collective-permute-start(s16[8,64,128]{2,1,0:T(8,128)(2,1)S(1)} %get-tuple-element.51), channel_id=1, source_target_pairs={{0,3},{1,2},{2,1},{3,0},{4,7},{5,6},{6,5},{7,4},{8,11},{9,10},{10,... | collective-permute-start | bytes 393224 | tf_op jit(solution)/shard_map/ppermute | solution.py:31
  95.3 12.2 %collective-permute-start.18 = (s16[8,64,128]{2,1,0:T(8,128)(2,1)S(1)}, s16[8,64,128]{2,1,0:T(8,128)(2,1)S(1)}, u32[]{:S(2)}, u32[]{:S(2)}) collective-permute-start(s16[8,64,128]{2,1,0:T(8,128)(2,1)S(1)} %get-tuple-element.41), channel_id=1, source_target_pairs={{0,16},{1,17},{2,18},{3,19},{4,20},{5,21},{6,22},{7,23},{8,24},{9,... | collective-permute-start | bytes 393224 | tf_op jit(solution)/shard_map/ppermute | solution.py:31
  97.4 10.1 %collective-permute-start.19 = (s16[8,64,128]{2,1,0:T(8,128)(2,1)S(1)}, s16[8,64,128]{2,1,0:T(8,128)(2,1)S(1)}, u32[]{:S(2)}, u32[]{:S(2)}) collective-permute-start(s16[8,64,128]{2,1,0:T(8,128)(2,1)S(1)} %get-tuple-element.42), channel_id=1, source_target_pairs={{0,32},{1,33},{2,34},{3,35},{4,36},{5,37},{6,38},{7,39},{8,40},{9,... | collective-permute-start | bytes 393224 | tf_op jit(solution)/shard_map/ppermute | solution.py:31
  98.9 8.6 %collective-permute-start.20 = (s16[8,64,128]{2,1,0:T(8,128)(2,1)S(1)}, s16[8,64,128]{2,1,0:T(8,128)(2,1)S(1)}, u32[]{:S(2)}, u32[]{:S(2)}) collective-permute-start(s16[8,64,128]{2,1,0:T(8,128)(2,1)S(1)} %get-tuple-element.43), channel_id=1, source_target_pairs={{0,48},{1,49},{2,50},{3,51},{4,52},{5,53},{6,54},{7,55},{8,56},{9,... | collective-permute-start | bytes 393224 | tf_op jit(solution)/shard_map/ppermute | solution.py:31
  107.6 8.5 %collective-permute-start.27 = (s16[128,128]{1,0:T(8,128)(2,1)S(1)}, s16[128,128]{1,0:T(8,128)(2,1)S(1)}, u32[]{:S(2)}, u32[]{:S(2)}) collective-permute-start(s16[128,128]{1,0:T(8,128)(2,1)S(1)} %get-tuple-element.53), channel_id=1, source_target_pairs={{0,4},{1,5},{2,6},{3,7},{4,0},{5,1},{6,2},{7,3},{8,12},{9,13},{10,... | collective-permute-start | bytes 98312 | tf_op jit(solution)/shard_map/ppermute | solution.py:31
  108.4 9.2 %collective-permute-start.28 = (s16[128,128]{1,0:T(8,128)(2,1)S(1)}, s16[128,128]{1,0:T(8,128)(2,1)S(1)}, u32[]{:S(2)}, u32[]{:S(2)}) collective-permute-start(s16[128,128]{1,0:T(8,128)(2,1)S(1)} %get-tuple-element.54), channel_id=1, source_target_pairs={{0,8},{1,9},{2,10},{3,11},{4,12},{5,13},{6,14},{7,15},{8,0},{9,1},... | collective-permute-start | bytes 98312 | tf_op jit(solution)/shard_map/ppermute | solution.py:31
  109.6 9.7 %collective-permute-start.29 = (s16[128,128]{1,0:T(8,128)(2,1)S(1)}, s16[128,128]{1,0:T(8,128)(2,1)S(1)}, u32[]{:S(2)}, u32[]{:S(2)}) collective-permute-start(s16[128,128]{1,0:T(8,128)(2,1)S(1)} %get-tuple-element.55), channel_id=1, source_target_pairs={{0,12},{1,13},{2,14},{3,15},{4,8},{5,9},{6,10},{7,11},{8,4},{9,5},... | collective-permute-start | bytes 98312 | tf_op jit(solution)/shard_map/ppermute | solution.py:31
  110.4 9.0 %collective-permute-start.30 = (s16[128,128]{1,0:T(8,128)(2,1)S(1)}, s16[128,128]{1,0:T(8,128)(2,1)S(1)}, u32[]{:S(2)}, u32[]{:S(2)}) collective-permute-start(s16[128,128]{1,0:T(8,128)(2,1)S(1)} %get-tuple-element.56), channel_id=1, source_target_pairs={{0,128},{1,129},{2,130},{3,131},{4,132},{5,133},{6,134},{7,135},{8... | collective-permute-start | bytes 98312 | tf_op jit(solution)/shard_map/ppermute | solution.py:31
  123.7 7.9 %collective-permute-start.38 = (bf16[128,128]{1,0:T(8,128)(2,1)S(1)}, bf16[128,128]{1,0:T(8,128)(2,1)S(1)}, u32[]{:S(2)}, u32[]{:S(2)}) collective-permute-start(bf16[128,128]{1,0:T(8,128)(2,1)S(1)} %get-tuple-element.61), channel_id=1, source_target_pairs={{0,4},{1,5},{2,6},{3,7},{4,0},{5,1},{6,2},{7,3},{8,12},{9,13},{10,... | collective-permute-start | bytes 98312 | tf_op jit(solution)/shard_map/ppermute | solution.py:31
  123.9 18.6 %collective-permute-start.39 = (bf16[128,128]{1,0:T(8,128)(2,1)S(1)}, bf16[128,128]{1,0:T(8,128)(2,1)S(1)}, u32[]{:S(2)}, u32[]{:S(2)}) collective-permute-start(bf16[128,128]{1,0:T(8,128)(2,1)S(1)} %get-tuple-element.61), channel_id=1, source_target_pairs={{0,8},{1,9},{2,10},{3,11},{4,12},{5,13},{6,14},{7,15},{8,0},{9,1},... | collective-permute-start | bytes 98312 | tf_op jit(solution)/shard_map/ppermute | solution.py:31
  125.8 19.5 %collective-permute-start.40 = (bf16[128,128]{1,0:T(8,128)(2,1)S(1)}, bf16[128,128]{1,0:T(8,128)(2,1)S(1)}, u32[]{:S(2)}, u32[]{:S(2)}) collective-permute-start(bf16[128,128]{1,0:T(8,128)(2,1)S(1)} %get-tuple-element.61), channel_id=1, source_target_pairs={{0,12},{1,13},{2,14},{3,15},{4,8},{5,9},{6,10},{7,11},{8,4},{9,5},... | collective-permute-start | bytes 98312 | tf_op jit(solution)/shard_map/ppermute | solution.py:31
  126.5 18.8 %collective-permute-start.41 = (bf16[128,128]{1,0:T(8,128)(2,1)S(1)}, bf16[128,128]{1,0:T(8,128)(2,1)S(1)}, u32[]{:S(2)}, u32[]{:S(2)}) collective-permute-start(bf16[128,128]{1,0:T(8,128)(2,1)S(1)} %get-tuple-element.61), channel_id=1, source_target_pairs={{0,128},{1,129},{2,130},{3,131},{4,132},{5,133},{6,134},{7,135},{8... | collective-permute-start | bytes 98312 | tf_op jit(solution)/shard_map/ppermute | solution.py:31
  128.7 16.7 %collective-permute-start.42 = (bf16[128,128]{1,0:T(8,128)(2,1)S(1)}, bf16[128,128]{1,0:T(8,128)(2,1)S(1)}, u32[]{:S(2)}, u32[]{:S(2)}) collective-permute-start(bf16[128,128]{1,0:T(8,128)(2,1)S(1)} %get-tuple-element.61), channel_id=1, source_target_pairs={{0,132},{1,133},{2,134},{3,135},{4,128},{5,129},{6,130},{7,131},{8... | collective-permute-start | bytes 98312 | tf_op jit(solution)/shard_map/ppermute | solution.py:31
  131.7 15.0 %collective-permute-start.43 = (bf16[128,128]{1,0:T(8,128)(2,1)S(1)}, bf16[128,128]{1,0:T(8,128)(2,1)S(1)}, u32[]{:S(2)}, u32[]{:S(2)}) collective-permute-start(bf16[128,128]{1,0:T(8,128)(2,1)S(1)} %get-tuple-element.61), channel_id=1, source_target_pairs={{0,136},{1,137},{2,138},{3,139},{4,140},{5,141},{6,142},{7,143},{8... | collective-permute-start | bytes 98312 | tf_op jit(solution)/shard_map/ppermute | solution.py:31
  142.5 6.0 %collective-permute-start.44 = (bf16[128,128]{1,0:T(8,128)(2,1)S(1)}, bf16[128,128]{1,0:T(8,128)(2,1)S(1)}, u32[]{:S(2)}, u32[]{:S(2)}) collective-permute-start(bf16[128,128]{1,0:T(8,128)(2,1)S(1)} %get-tuple-element.61), channel_id=1, source_target_pairs={{0,140},{1,141},{2,142},{3,143},{4,136},{5,137},{6,138},{7,139},{8... | collective-permute-start | bytes 98312 | tf_op jit(solution)/shard_map/ppermute | solution.py:31
  148.7 7.2 %collective-permute-start.56 = (bf16[8,64,128]{2,1,0:T(8,128)(2,1)S(1)}, bf16[8,64,128]{2,1,0:T(8,128)(2,1)S(1)}, u32[]{:S(2)}, u32[]{:S(2)}) collective-permute-start(bf16[8,64,128]{2,1,0:T(8,128)(2,1)S(1)} %get-tuple-element.66), channel_id=1, source_target_pairs={{0,2},{1,3},{2,0},{3,1},{4,6},{5,7},{6,4},{7,5},{8,10},{9,11},{10,... | collective-permute-start | bytes 393224 | tf_op jit(solution)/shard_map/ppermute | solution.py:31
  152.6 6.1 %collective-permute-start.45 = (bf16[8,64,128]{2,1,0:T(8,128)(2,1)S(1)}, bf16[8,64,128]{2,1,0:T(8,128)(2,1)S(1)}, u32[]{:S(2)}, u32[]{:S(2)}) collective-permute-start(bf16[8,64,128]{2,1,0:T(8,128)(2,1)S(1)} %get-tuple-element.67), channel_id=1, source_target_pairs={{0,16},{1,17},{2,18},{3,19},{4,20},{5,21},{6,22},{7,23},{8,24},{9,... | collective-permute-start | bytes 393224 | tf_op jit(solution)/shard_map/ppermute | solution.py:31
  154.1 5.9 %collective-permute-start.46 = (bf16[8,64,128]{2,1,0:T(8,128)(2,1)S(1)}, bf16[8,64,128]{2,1,0:T(8,128)(2,1)S(1)}, u32[]{:S(2)}, u32[]{:S(2)}) collective-permute-start(bf16[8,64,128]{2,1,0:T(8,128)(2,1)S(1)} %get-tuple-element.67), channel_id=1, source_target_pairs={{0,32},{1,33},{2,34},{3,35},{4,36},{5,37},{6,38},{7,39},{8,40},{9,... | collective-permute-start | bytes 393224 | tf_op jit(solution)/shard_map/ppermute | solution.py:31
  156.9 70.5 %collective-permute-start.59 = (bf16[4,8,64,128]{3,2,1,0:T(8,128)(2,1)S(1)}, bf16[4,8,64,128]{3,2,1,0:T(8,128)(2,1)S(1)}, u32[]{:S(2)}, u32[]{:S(2)}) collective-permute-start(bf16[4,8,64,128]{3,2,1,0:T(8,128)(2,1)S(1)} %pad_maximum_fusion.1.refs_4_), channel_id=1, source_target_pairs={{0,16},{1,17},{2,18},{3,19},{4,20},{5,21},{6,22},{7,23},{8,24},{9,... | collective-permute-start | bytes 1572872 | tf_op jit(solution)/shard_map/ppermute | solution.py:31
  158.7 70.1 %collective-permute-start.61 = (bf16[4,8,64,128]{3,2,1,0:T(8,128)(2,1)S(1)}, bf16[4,8,64,128]{3,2,1,0:T(8,128)(2,1)S(1)}, u32[]{:S(2)}, u32[]{:S(2)}) collective-permute-start(bf16[4,8,64,128]{3,2,1,0:T(8,128)(2,1)S(1)} %pad_maximum_fusion.1.refs_4_), channel_id=1, source_target_pairs={{0,32},{1,33},{2,34},{3,35},{4,36},{5,37},{6,38},{7,39},{8,40},{9,... | collective-permute-start | bytes 1572872 | tf_op jit(solution)/shard_map/ppermute | solution.py:31
  158.7 74.7 %collective-permute-start.63 = (bf16[4,8,64,128]{3,2,1,0:T(8,128)(2,1)S(1)}, bf16[4,8,64,128]{3,2,1,0:T(8,128)(2,1)S(1)}, u32[]{:S(2)}, u32[]{:S(2)}) collective-permute-start(bf16[4,8,64,128]{3,2,1,0:T(8,128)(2,1)S(1)} %pad_maximum_fusion.1.refs_4_), channel_id=1, source_target_pairs={{0,48},{1,49},{2,50},{3,51},{4,52},{5,53},{6,54},{7,55},{8,56},{9,... | collective-permute-start | bytes 1572872 | tf_op jit(solution)/shard_map/ppermute | solution.py:31
  160.1 73.5 %collective-permute-start.49 = (bf16[4,8,64,128]{3,2,1,0:T(8,128)(2,1)S(1)}, bf16[4,8,64,128]{3,2,1,0:T(8,128)(2,1)S(1)}, u32[]{:S(2)}, u32[]{:S(2)}) collective-permute-start(bf16[4,8,64,128]{3,2,1,0:T(8,128)(2,1)S(1)} %pad_maximum_fusion.refs_0_), channel_id=1, source_target_pairs={{0,1},{1,0},{2,3},{3,2},{4,5},{5,4},{6,7},{7,6},{8,9},{9,8},{10,11... | collective-permute-start | bytes 1572872 | tf_op jit(solution)/shard_map/ppermute | solution.py:31
  160.8 28.6 %collective-permute-start.35 = (f32[32,128]{1,0:T(8,128)S(1)}, f32[32,128]{1,0:T(8,128)S(1)}, u32[]{:S(2)}, u32[]{:S(2)}) collective-permute-start(f32[32,128]{1,0:T(8,128)S(1)} %get-tuple-element.71), channel_id=1, source_target_pairs={{0,64},{1,0},{2,192},{3,128},{4,68},{5,4},{6,196},{7,132},{8,72},{... | collective-permute-start | bytes 49160 | tf_op jit(solution)/shard_map/ppermute | solution.py:266
  189.4 10.4 %collective-permute-start.36 = (f32[32,128]{1,0:T(8,128)S(1)}, f32[32,128]{1,0:T(8,128)S(1)}, u32[]{:S(2)}, u32[]{:S(2)}) collective-permute-start(f32[32,128]{1,0:T(8,128)S(1)} %get-tuple-element.70), channel_id=1, source_target_pairs={{0,128},{1,192},{2,0},{3,64},{4,132},{5,196},{6,4},{7,68},{8,136},... | collective-permute-start | bytes 49160 | tf_op jit(solution)/shard_map/ppermute | solution.py:266
  199.8 16.9 %collective-permute-start.37 = (f32[32,128]{1,0:T(8,128)S(1)}, f32[32,128]{1,0:T(8,128)S(1)}, u32[]{:S(2)}, u32[]{:S(2)}) collective-permute-start(f32[32,128]{1,0:T(8,128)S(1)} %get-tuple-element.69), channel_id=1, source_target_pairs={{0,192},{1,128},{2,64},{3,0},{4,196},{5,132},{6,68},{7,4},{8,200},... | collective-permute-start | bytes 49160 | tf_op jit(solution)/shard_map/ppermute | solution.py:266
  216.7 10.8 %collective-permute-start.34 = (f32[32,128]{1,0:T(8,128)S(1)}, f32[32,128]{1,0:T(8,128)S(1)}, u32[]{:S(2)}, u32[]{:S(2)}) collective-permute-start(f32[32,128]{1,0:T(8,128)S(1)} %get-tuple-element.68), channel_id=1, source_target_pairs={{0,0},{1,64},{2,128},{3,192},{4,4},{5,68},{6,132},{7,196},{8,8},{9... | collective-permute-start | bytes 49160 | tf_op jit(solution)/shard_map/ppermute | solution.py:266
  227.4 14.5 %collective-permute-start.51 = (bf16[4,8,64,128]{3,2,1,0:T(8,128)(2,1)S(1)}, bf16[4,8,64,128]{3,2,1,0:T(8,128)(2,1)}, u32[]{:S(2)}, u32[]{:S(2)}) collective-permute-start(bf16[4,8,64,128]{3,2,1,0:T(8,128)(2,1)S(1)} %pad_maximum_fusion.refs_0_), channel_id=1, source_target_pairs={{0,2},{1,3},{2,0},{3,1},{4,6},{5,7},{6,4},{7,5},{8,10},{9,11},{10,... | collective-permute-start | bytes 1572872 | tf_op jit(solution)/shard_map/ppermute | solution.py:31
  227.4 25.8 %collective-permute-start.53 = (bf16[4,8,64,128]{3,2,1,0:T(8,128)(2,1)S(1)}, bf16[4,8,64,128]{3,2,1,0:T(8,128)(2,1)}, u32[]{:S(2)}, u32[]{:S(2)}) collective-permute-start(bf16[4,8,64,128]{3,2,1,0:T(8,128)(2,1)S(1)} %pad_maximum_fusion.refs_0_), channel_id=1, source_target_pairs={{0,3},{1,2},{2,1},{3,0},{4,7},{5,6},{6,5},{7,4},{8,11},{9,10},{10,... | collective-permute-start | bytes 1572872 | tf_op jit(solution)/shard_map/ppermute | solution.py:31
  228.8 25.0 %collective-permute-start.58 = (bf16[4,8,64,128]{3,2,1,0:T(8,128)(2,1)S(1)}, bf16[4,8,64,128]{3,2,1,0:T(8,128)(2,1)}, u32[]{:S(2)}, u32[]{:S(2)}) collective-permute-start(bf16[4,8,64,128]{3,2,1,0:T(8,128)(2,1)S(1)} %pad_maximum_fusion.1.refs_4_), channel_id=1, source_target_pairs={{0,64},{1,65},{2,66},{3,67},{4,68},{5,69},{6,70},{7,71},{8,72},{9,... | collective-permute-start | bytes 1572872 | tf_op jit(solution)/shard_map/ppermute | solution.py:31
  233.5 20.3 %collective-permute-start.48 = (bf16[4,8,64,128]{3,2,1,0:T(8,128)(2,1)S(1)}, bf16[4,8,64,128]{3,2,1,0:T(8,128)(2,1)}, u32[]{:S(2)}, u32[]{:S(2)}) collective-permute-start(bf16[4,8,64,128]{3,2,1,0:T(8,128)(2,1)S(1)} %pad_maximum_fusion.refs_0_), channel_id=1, source_target_pairs={{0,64},{1,65},{2,66},{3,67},{4,68},{5,69},{6,70},{7,71},{8,72},{9,... | collective-permute-start | bytes 1572872 | tf_op jit(solution)/shard_map/ppermute | solution.py:31
  233.6 20.7 %collective-permute-start.60 = (bf16[4,8,64,128]{3,2,1,0:T(8,128)(2,1)S(1)}, bf16[4,8,64,128]{3,2,1,0:T(8,128)(2,1)}, u32[]{:S(2)}, u32[]{:S(2)}) collective-permute-start(bf16[4,8,64,128]{3,2,1,0:T(8,128)(2,1)S(1)} %collective-permute-done.59.refs_5_), channel_id=1, source_target_pairs={{0,64},{1,65},{2,66},{3,67},{4,68},{5,69},{6,70},{7,71},{8,72},{9,... | collective-permute-start | bytes 1572872 | tf_op jit(solution)/shard_map/ppermute | solution.py:31
  241.9 20.5 %collective-permute-start.62 = (bf16[4,8,64,128]{3,2,1,0:T(8,128)(2,1)S(1)}, bf16[4,8,64,128]{3,2,1,0:T(8,128)(2,1)}, u32[]{:S(2)}, u32[]{:S(2)}) collective-permute-start(bf16[4,8,64,128]{3,2,1,0:T(8,128)(2,1)S(1)} %collective-permute-done.61.refs_6_), channel_id=1, source_target_pairs={{0,64},{1,65},{2,66},{3,67},{4,68},{5,69},{6,70},{7,71},{8,72},{9,... | collective-permute-start | bytes 1572872 | tf_op jit(solution)/shard_map/ppermute | solution.py:31
  253.3 9.2 %collective-permute-start.64 = (bf16[4,8,64,128]{3,2,1,0:T(8,128)(2,1)S(1)}, bf16[4,8,64,128]{3,2,1,0:T(8,128)(2,1)}, u32[]{:S(2)}, u32[]{:S(2)}) collective-permute-start(bf16[4,8,64,128]{3,2,1,0:T(8,128)(2,1)S(1)} %collective-permute-done.63.refs_7_), channel_id=1, source_target_pairs={{0,64},{1,65},{2,66},{3,67},{4,68},{5,69},{6,70},{7,71},{8,72},{9,... | collective-permute-start | bytes 1572872 | tf_op jit(solution)/shard_map/ppermute | solution.py:31
  253.8 8.7 %collective-permute-start.50 = (bf16[4,8,64,128]{3,2,1,0:T(8,128)(2,1)S(1)}, bf16[4,8,64,128]{3,2,1,0:T(8,128)(2,1)}, u32[]{:S(2)}, u32[]{:S(2)}) collective-permute-start(bf16[4,8,64,128]{3,2,1,0:T(8,128)(2,1)S(1)} %collective-permute-done.49.refs_1_), channel_id=1, source_target_pairs={{0,64},{1,65},{2,66},{3,67},{4,68},{5,69},{6,70},{7,71},{8,72},{9,... | collective-permute-start | bytes 1572872 | tf_op jit(solution)/shard_map/ppermute | solution.py:31
  253.8 8.7 %collective-permute-start.52 = (bf16[4,8,64,128]{3,2,1,0:T(8,128)(2,1)}, bf16[4,8,64,128]{3,2,1,0:T(8,128)(2,1)}, u32[]{:S(2)}, u32[]{:S(2)}) collective-permute-start(bf16[4,8,64,128]{3,2,1,0:T(8,128)(2,1)} %collective-permute-done.51.refs_2_), channel_id=1, source_target_pairs={{0,64},{1,65},{2,66},{3,67},{4,68},{5,69},{6,70},{7,71},{8,72},{9,... | collective-permute-start | bytes 1572872 | tf_op jit(solution)/shard_map/ppermute | solution.py:31
  254.3 8.2 %collective-permute-start.54 = (bf16[4,8,64,128]{3,2,1,0:T(8,128)(2,1)}, bf16[4,8,64,128]{3,2,1,0:T(8,128)(2,1)}, u32[]{:S(2)}, u32[]{:S(2)}) collective-permute-start(bf16[4,8,64,128]{3,2,1,0:T(8,128)(2,1)} %collective-permute-done.53.refs_3_), channel_id=1, source_target_pairs={{0,64},{1,65},{2,66},{3,67},{4,68},{5,69},{6,70},{7,71},{8,72},{9,... | collective-permute-start | bytes 1572872 | tf_op jit(solution)/shard_map/ppermute | solution.py:31
  (20 other events, 254.3 us)

commit v2 on v0

v2 whole, which is shorter than its diff:
```python
import functools

import jax
import jax.numpy as jnp
from jax import lax
from jax.experimental import pallas as pl
from jax.experimental.pallas import tpu as pltpu
from jax.sharding import PartitionSpec as P

AXES = ("outer", "dp")
NX, NY, NZ, NC = 4, 4, 8, 2
PASS = 128
VMEM = 16 * 1024 * 1024


def coords(index):
    outer, dp = divmod(index, 64)
    return (outer // 2) * 4 + dp // 4 % 4, dp // 16, dp % 4, outer % 2


def linear(z, y, x, c):
    return ((z // 4) * 2 + c) * 64 + (y * 4 + z % 4) * 4 + x


def swap(array, z=0, y=0, x=0, c=0):
    pairs = []
    for index in range(256):
        at = coords(index)
        pairs.append((index, linear(at[0] ^ z, at[1] ^ y, at[2] ^ x, at[3] ^ c)))
    return lax.ppermute(array, AXES, pairs)


def exchange(array, varies):
    groups = {}
    for index in range(256):
        fixed = tuple(at for at, name in zip(coords(index), "zyxc") if name not in varies)
        groups.setdefault(fixed, []).append(index)
    return lax.all_to_all(array, AXES, 0, 0, tiled=True, axis_index_groups=list(groups.values()))


def hadamard(length):
    index_row = jnp.arange(length, dtype=jnp.int32)[:, None]
    index_col = jnp.arange(length, dtype=jnp.int32)[None, :]
    common_bits = index_row & index_col
    parity = jnp.zeros((length, length), jnp.int32)
    for bit_pos in range(length.bit_length() - 1):
        parity = parity + (common_bits >> bit_pos & 1)
    return (1 - 2 * (parity % 2)).astype(jnp.float32)


def split3(value):
    high = value.astype(jnp.bfloat16)
    rest = value - high.astype(jnp.float32)
    mid = rest.astype(jnp.bfloat16)
    low = (rest - mid.astype(jnp.float32)).astype(jnp.bfloat16)
    return high, mid, low


def dot(a, b):
    return jnp.dot(a, b, preferred_element_type=jnp.float32)


def params():
    return pltpu.CompilerParams(vmem_limit_bytes=VMEM)


def cost(flops, nbytes):
    return pl.CostEstimate(flops=flops, bytes_accessed=nbytes, transcendentals=0)


def rotate_kernel(core_ref, x_ref, sign_ref, h_ref, out_ref, max_ref):
    h = h_ref[...]
    sign = sign_ref[...]
    peak = jnp.zeros((8, PASS), jnp.float32)
    flipped = [x_ref[0, z % 4, 0, z // 4, 0] * sign for z in range(NZ)]
    first = dot(jnp.concatenate(flipped, axis=0), h)
    high, mid, low = split3(first)
    for z in range(NZ):
        rows = slice(z * PASS, (z + 1) * PASS)
        turned = (dot(h, high[rows]) + (dot(h, mid[rows]) + dot(h, low[rows]))) * (1.0 / PASS)
        out_ref[z] = turned
        peak = jnp.maximum(peak, jnp.max(jnp.abs(turned).reshape(16, 8, PASS), axis=0))

    @pl.when((pl.program_id(0) == 0) & (pl.program_id(1) == 0))
    def _():
        max_ref[...] = jnp.zeros_like(max_ref)

    max_ref[...] = jnp.maximum(max_ref[...], peak)


def bucket_spec(core):
    return pl.BlockSpec((1, 4, 1, 2, 1, PASS, PASS), lambda y, x, at: (y, 0, x, 0, core(at), 0, 0))


def rotate(blocks, core, sign, h):
    return pl.pallas_call(
        rotate_kernel,
        grid_spec=pltpu.PrefetchScalarGridSpec(
            num_scalar_prefetch=1,
            grid=(NY, NX),
            in_specs=[
                bucket_spec(lambda at: at[0]),
                pl.BlockSpec((PASS, PASS), lambda y, x, at: (0, 0)),
                pl.BlockSpec((PASS, PASS), lambda y, x, at: (0, 0)),
            ],
            out_specs=[
                pl.BlockSpec((NZ, PASS, PASS), lambda y, x, at: (y * NX + x, 0, 0)),
                pl.BlockSpec((8, PASS), lambda y, x, at: (0, 0)),
            ],
        ),
        out_shape=[
            pltpu.VMEM((128, PASS, PASS), jnp.float32),
            jax.ShapeDtypeStruct((8, PASS), jnp.float32),
        ],
        compiler_params=params(),
        cost_estimate=cost(8 * 128 * PASS**3, 12 << 20),
        name="rotate",
    )(core, blocks, sign, h)


GROUPS = 4


def hops(group):
    return ("x", "y") if group < 2 else ("y", "x"), (1, 3) if group % 2 == 0 else (3, 1)


def orders(group, y, x):
    axes, (a, b) = hops(group)
    at = {"y": y, "x": x}
    first = at[axes[0]] ^ jnp.array([a, 2, 0, b], jnp.int32)
    second = at[axes[1]] ^ jnp.array([0, b, a, 2], jnp.int32)
    return jnp.concatenate([first, second])


def quantize_kernel(group, at_ref, max_ref, own_ref, mate_ref, sent_ref, kept_ref):
    scale = 127.0 / jnp.max(max_ref[...])

    for out_ref, start in ((sent_ref, 0), (kept_ref, 2)):
        for i in range(2):
            for j in range(4):
                first, second = at_ref[group, start + i], at_ref[group, 4 + j]
                y, x = (second, first) if group < 2 else (first, second)
                for k in range(2):
                    b = (y * NX + x) * NZ + 2 * group + k
                    code = jnp.floor(own_ref[b] * scale + 0.5) + jnp.floor(mate_ref[b] * scale + 0.5)
                    out_ref[i, j, k] = code.astype(jnp.bfloat16)


def in_vmem(array):
    return pltpu.with_memory_space_constraint(array, pltpu.VMEM)


def quantize(group, table, maximum, own, mate):
    vmem = pl.BlockSpec(memory_space=pltpu.VMEM)
    return pl.pallas_call(
        functools.partial(quantize_kernel, group),
        in_specs=[pl.BlockSpec(memory_space=pltpu.SMEM), vmem, vmem, vmem],
        out_specs=[vmem, vmem],
        out_shape=[jax.ShapeDtypeStruct((2, 4, 2, PASS, PASS), jnp.bfloat16)] * 2,
        compiler_params=params(),
        cost_estimate=cost(1 << 22, 5 << 20),
        name="quantize",
    )(table, maximum, own, mate)


def add_kernel(kept_ref, got_ref, low_ref, high_ref):
    count = low_ref.shape[0]
    halves = ((0, low_ref), (count, high_ref)) if len(kept_ref.shape) == len(low_ref.shape) else ((0, low_ref), (1, high_ref))
    for start, out_ref in halves:
        at = pl.ds(start, count) if len(kept_ref.shape) == len(low_ref.shape) else start
        total = kept_ref[at].astype(jnp.int32) + got_ref[at].astype(jnp.int32)
        out_ref[...] = total.astype(jnp.int16)


def add_two(kept, got, shape):
    return pl.pallas_call(
        add_kernel,
        out_shape=[jax.ShapeDtypeStruct(shape, jnp.int16)] * 2,
        compiler_params=params(),
        cost_estimate=cost(kept.size, kept.size * 6),
        name="add_two",
    )(kept, got)


def add_last_kernel(*refs):
    for g in range(GROUPS):
        total = refs[2 * g][...].astype(jnp.int32) + refs[2 * g + 1][...].astype(jnp.int32)
        refs[-1][2 * g : 2 * g + 2] = total.astype(jnp.int16)


def add_last(terms):
    return pl.pallas_call(
        add_last_kernel,
        out_shape=jax.ShapeDtypeStruct((NZ, PASS, PASS), jnp.int16),
        compiler_params=params(),
        cost_estimate=cost(1 << 18, 3 << 18),
        name="add_last",
    )(*terms)


def reduce_plane(table, maximum, own, mate):
    parts = [quantize(g, table, maximum, own, mate) for g in range(GROUPS)]
    for axis in range(2):
        for hop in range(2):
            got = []
            for g in range(GROUPS):
                axes, xors = hops(g)
                got.append(swap(parts[g][0], **{axes[axis]: xors[hop]}))
            if axis == 1 and hop == 1:
                return add_last([t for g in range(GROUPS) for t in (parts[g][1], got[g])])
            if hop == 0:
                shape = parts[0][1].shape[1:]
                parts = [add_two(parts[g][1], got[g], shape)[::-1] for g in range(GROUPS)]
            else:
                shape = (2, *parts[0][1].shape[1:])
                parts = [add_two(parts[g][1], got[g], shape)[::-1] for g in range(GROUPS)]


def gather_plane(line):
    held = [line[2 * g : 2 * g + 2][None] for g in range(GROUPS)]
    for axis in (1, 0):
        for hop in (1, 0):
            got = []
            for g in range(GROUPS):
                axes, xors = hops(g)
                got.append(swap(held[g], **{axes[axis]: xors[hop]}))
            if axis == 0 and hop == 0:
                return [pair for g in range(GROUPS) for pair in (held[g], got[g])]
            held = [jnp.concatenate([held[g], got[g]], axis=0) for g in range(GROUPS)]
        held = [h[None] for h in held]


def assemble_kernel(*refs):
    at_ref, pieces, out_ref, sems = refs[0], refs[1:9], refs[-2], refs[-1]
    copies = []
    for g in range(GROUPS):
        for part in range(2):
            for i in range(2):
                for j in range(4):
                    first = at_ref[g, 2 + i if part == 0 else i]
                    second = at_ref[g, 4 + j]
                    y, x = (second, first) if g < 2 else (first, second)
                    z = 2 * g
                    copies.append(
                        pltpu.make_async_copy(
                            pieces[2 * g + part].at[i, j],
                            out_ref.at[y, pl.ds(z % 4, 2), x, z // 4, at_ref[GROUPS, 0]],
                            sems.at[len(copies)],
                        )
                    )
    for copy in copies:
        copy.start()
    for copy in copies:
        copy.wait()


def assemble(at, pieces, before=None):
    more = [] if before is None else [before]
    anywhere = pl.BlockSpec(memory_space=pl.ANY)
    return pl.pallas_call(
        assemble_kernel,
        in_specs=[pl.BlockSpec(memory_space=pltpu.SMEM)]
        + [pl.BlockSpec(memory_space=pltpu.VMEM)] * 8
        + [anywhere] * len(more),
        out_specs=anywhere,
        out_shape=jax.ShapeDtypeStruct((NY, 4, NX, 2, NC, PASS, PASS), jnp.bfloat16),
        scratch_shapes=[pltpu.SemaphoreType.DMA((64,))],
        input_output_aliases={9: 0} if more else {},
        compiler_params=params(),
        cost_estimate=cost(1 << 10, 8 << 20),
        name="assemble",
    )(at, *pieces, *more)


def all_max(value):
    value = jnp.max(exchange(jnp.broadcast_to(value[None], (NZ * NC, *value.shape)), "zc"), axis=0)
    return jnp.max(exchange(jnp.broadcast_to(value[None], (NY * NX, *value.shape)), "yx"), axis=0)


def decode_kernel(max_ref, sign_ref, h_ref, terms_ref, total_ref, out_ref):
    total = terms_ref[0].astype(jnp.int32)
    for k in range(1, NZ):
        total = total + terms_ref[k].astype(jnp.int32)
    total = total.astype(jnp.float32)
    total_ref[...] = total
    h = h_ref[...]
    high, mid, low = split3(total)
    first = dot(high, h) + (dot(mid, h) + dot(low, h))
    high, mid, low = split3(first)
    second = dot(h, high) + (dot(h, mid) + dot(h, low))
    unit = jnp.max(max_ref[...]) / (127.0 * PASS)
    decoded = (second * sign_ref[...].astype(jnp.float32) * unit).astype(jnp.bfloat16)
    for k in range(NZ):
        out_ref[k] = decoded


def decode(maximum, sign, h, terms):
    return pl.pallas_call(
        decode_kernel,
        out_shape=[
            jax.ShapeDtypeStruct((PASS, PASS), jnp.float32),
            jax.ShapeDtypeStruct((NZ, PASS, PASS), jnp.bfloat16),
        ],
        compiler_params=params(),
        cost_estimate=cost(12 * PASS**3, 1 << 19),
        name="decode",
    )(maximum, sign, h, terms)


def pick(pair, index):
    return jnp.where(index == 0, pair[0], pair[1])


def mean_rows(total, z_high, c):
    rows = (total / 256.0).reshape(2, 2, PASS // 4, PASS)
    kept, sent = pick(rows, z_high), pick(rows, 1 - z_high)
    got = swap(sent, z=4)
    both = jnp.where(z_high == 0, jnp.stack([kept, got]), jnp.stack([got, kept]))
    both = jnp.swapaxes(both, 0, 1)
    kept, sent = pick(both, c), pick(both, 1 - c)
    got = swap(sent, c=1)
    both = jnp.where(c == 0, jnp.stack([kept, got], axis=1), jnp.stack([got, kept], axis=1))
    return both.reshape(4, PASS // 4, PASS)


def body(gradients, sign_flips):
    outer, dp = lax.axis_index("outer"), lax.axis_index("dp")
    z_high, c = outer // 2, outer % 2
    y, x = dp // 16, dp % 4
    bucket = gradients.reshape(NY, 4, NX, 2, NC, PASS, PASS)
    h = hadamard(PASS).astype(jnp.bfloat16)
    sign = sign_flips.astype(jnp.bfloat16)
    here = jnp.stack([c]).astype(jnp.int32)

    mates = swap(lax.dynamic_slice_in_dim(bucket, 1 - c, 1, 4), c=1)
    own, own_max = rotate(bucket, here, sign, h)
    mate, mate_max = rotate(mates, jnp.zeros((1,), jnp.int32), sign, h)
    maximum = all_max(jnp.maximum(own_max, mate_max))

    table = jnp.stack([orders(g, y, x) for g in range(GROUPS)])
    terms = exchange(reduce_plane(table, maximum, in_vmem(own), in_vmem(mate)), "z")
    total, decoded = decode(maximum, sign, h, terms)
    mean = mean_rows(total, z_high, c)

    pieces = gather_plane(exchange(decoded, "z"))
    mates = [swap(piece, c=1) for piece in pieces]
    gradient_sum = assemble(jnp.concatenate([table, jnp.full((1, 8), c, jnp.int32)]), pieces)
    gradient_sum = assemble(jnp.concatenate([table, jnp.full((1, 8), 1 - c, jnp.int32)]), mates, gradient_sum)
    return (mean, gradient_sum.reshape(256, PASS, PASS))


def solution(mesh):
    placed = (P("outer", "dp", None, None, None), P())
    return jax.shard_map(
        body, mesh=mesh, in_specs=placed, out_specs=(P("dp", "outer", None), P()), check_vma=False
    )
```

time: 971 us -> 204 us (0.21)
  waiting for transfers between devices: 811 us -> 58.8 us
  blocking collectives: 78.6 us -> 12.9 us
  starting transfers between devices: 0.3 us -> 64.8 us
  matrix products: 38.7 us -> 0 us
  Pallas kernels: 0 us -> 37.7 us
  between operations: 15.1 us -> 1.4 us
  other arithmetic: 14.1 us -> 0.88 us
  local copies, waits for them, and re-layouts: 12.1 us -> 25.3 us
    reduce_scatter x1 -> x0, waiting for transfers between devices: 401 us -> none  [body(): lax.psum_scatter(code_terms, 'dp', scatter_dimension=0, tiled=True)]
    all_gather x1 -> x0, waiting for transfers between devices: 355 us -> none  [body(): gradient_sum = lax.all_gather(decoded_local, 'dp', axis=0, tiled=True)]
    pmax x1 -> x0, blocking collectives: 78.6 us -> none  [body(): maximum = lax.pmax(jnp.max(jnp.abs(rotated)), ('outer', 'dp'))]
    psum x1 -> x0, waiting for transfers between devices: 55.3 us -> none  [body(): code_total = lax.psum(pod_share, 'outer')]
    ppermute x0 -> x43, starting transfers between devices: none -> 45.2 us  [swap(): return lax.ppermute(array, AXES, pairs)]
    ppermute x0 -> x43, waiting for transfers between devices: none -> 40.3 us  [swap(): return lax.ppermute(array, AXES, pairs)]
    dot_general x4 -> x0, matrix products: 38.7 us -> none  [the longest x1 20.3 us: rotate(): jnp.einsum('bij,jk->bik', flipped, hadamard_mat, precision=lax.Precision....]
    pallas_call x0 -> x22, Pallas kernels: none -> 37.7 us  [the longest x2 21.9 us: rotate(): pl.pallas_call(rotate_kernel, grid_spec=pltpu.PrefetchScalarGridSpec(num_...]
  transfers between devices with their start and end apart: 3 -> 46, of which waited for: 3 -> 22; matrix products, arithmetic and copies ran while one was open for 0% -> 1% of each run, Pallas kernels for 0% -> 8%
where the time goes in v2:
time: 204 us; the launch traced here: 202 us
  starting transfers between devices  64.8 us (32%)
  waiting for transfers between devices  58.8 us (29%)
  Pallas kernels  37.7 us (18%)
  local copies, waits for them, and re-layouts  25.3 us (12%)
  blocking collectives  12.9 us (6%)
    ppermute x43, starting transfers between devices, swap(): return lax.ppermute(array, AXES, pairs)  45.2 us
    ppermute x43, waiting for transfers between devices, swap(): return lax.ppermute(array, AXES, pairs)  40.3 us
    pallas_call x2, Pallas kernels, rotate(): pl.pallas_call(rotate_kernel, grid_spec=pltpu.PrefetchScalarGridSpec(num_...  21.9 us
    all_to_all x3, starting transfers between devices, exchange(): lax.all_to_all(array, AXES, 0, 0, tiled=True, axis_index_groups=list(grou...  19.6 us
    unnamed x28, local copies, waits for them, and re-layouts  18.5 us
    all_to_all x3, waiting for transfers between devices, exchange(): lax.all_to_all(array, AXES, 0, 0, tiled=True, axis_index_groups=list(grou...  18.5 us
    all_to_all x1, blocking collectives, exchange(): lax.all_to_all(array, AXES, 0, 0, tiled=True, axis_index_groups=list(grou...  12.9 us
    pallas_call x2, Pallas kernels, assemble(): pl.pallas_call(assemble_kernel, in_specs=[pl.BlockSpec(memory_space=pltpu...  8.12 us
  transfers between devices with their start and end apart: 46, of which 22 were waited for; matrix products, arithmetic and copies ran while one was open for 1% of the time, Pallas kernels for 8%

profile of v2, /device:TPU:2, one launch (start us, length us, event | category | flops | bytes accessed | tf_op | source)
XLA Modules:
  0.0 201.7 jit_solution(15342103856372297972)
XLA Ops:
  0.7 4.8 %constant_dynamic-slice_fusion = bf16[4,4,4,2,1,128,128]{6,5,4,3,2,1,0:T(8,128)(2,1)} fusion(bf16[4,4,4,2,2,128,128]{6,5,4,3,2,1,0:T(8,128)(2,1)} %bitcast.46, s32[]{:T(128)S(6)} %select_n.108), kind=kLoop, calls=%fused_computation.46 | loop fusion | bytes 8388612 | tf_op jit(solution)/shard_map/dynamic_slice | solution.py:336
  5.9 3.4 %copy-done.4 = bf16[1,1,256,128,128]{4,3,2,1,0:T(8,128)(2,1)S(1)} copy-done((bf16[1,1,256,128,128]{4,3,2,1,0:T(8,128)(2,1)S(1)}, bf16[1,1,256,128,128]{4,3,2,1,0:T(8,128)(2,1)}, u32[]{:S(2)}) %copy-start.4) | copy-done | bytes 8388632
  9.3 9.2 %rotate.2 = (f32[128,128,128]{2,1,0:T(8,128)S(1)}, f32[8,128]{1,0:T(8,128)S(1)}) custom-call(s32[1]{0:T(128)} %bitcast.core_ref, bf16[4,4,4,2,2,128,128]{6,5,4,3,2,1,0:T(8,128)(2,1)S(1)} %bitcast.47, bf16[128,128]{1,0:T(8,128)(2,1)S(1)} %convert_element_type.17.sign_ref, bf16[128,128]{1,0:T(8,128)(2,1)S(1)} %fusion.4.h_ref), custom_call_target="tpu_custom_call" | custom-call | flops 2147483648 | bytes 12582912 | tf_op jit(solution)/shard_map/rotate/pallas_call | solution.py:96
  18.5 3.4 %copy-done = f32[128,128,128]{2,1,0:T(8,128)} copy-done((f32[128,128,128]{2,1,0:T(8,128)}, f32[128,128,128]{2,1,0:T(8,128)S(1)}, u32[]{:S(2)}) %copy-start) | copy-done | bytes 8388632
  21.8 12.7 %rotate.3 = (f32[128,128,128]{2,1,0:T(8,128)S(1)}, f32[8,128]{1,0:T(8,128)S(1)}) custom-call(s32[1]{0:T(128)} %constant.83.clone.1.core_ref, bf16[4,4,4,2,1,128,128]{6,5,4,3,2,1,0:T(8,128)(2,1)} %collective-permute-done.x_ref, bf16[128,128]{1,0:T(8,128)(2,1)S(1)} %convert_element_type.17.sign_ref, bf16[128,128]{1,0:T(8,128)(2,1)S(1)} %fusion.4.h_ref), custom_call_target="tpu_custom_call" | custom-call | flops 2147483648 | bytes 12582912 | tf_op jit(solution)/shard_map/rotate/pallas_call | solution.py:96
  34.6 3.3 %copy-done.2 = f32[128,128,128]{2,1,0:T(8,128)} copy-done((f32[128,128,128]{2,1,0:T(8,128)}, f32[128,128,128]{2,1,0:T(8,128)S(1)}, u32[]{:S(2)}) %copy-start.2) | copy-done | bytes 8388632
  38.6 8.7 %all-to-all-start = ((f32[16,8,128]{2,1,0:T(8,128)}), f32[16,8,128]{2,1,0:T(8,128)S(1)}, u32[]{:S(2)}, u32[]{:S(2)}) async-start(f32[16,8,128]{2,1,0:T(8,128)} %broadcast_in_dim.44), calls=%async_computation | async-start | bytes 131072 | tf_op jit(solution)/shard_map/all_to_all | solution.py:38
  47.4 7.7 %all-to-all-done = f32[16,8,128]{2,1,0:T(8,128)S(1)} async-done(((f32[16,8,128]{2,1,0:T(8,128)}), f32[16,8,128]{2,1,0:T(8,128)S(1)}, u32[]{:S(2)}, u32[]{:S(2)}) %all-to-all-start) | async-done | bytes 65568 | tf_op jit(solution)/shard_map/all_to_all | solution.py:38
  55.8 7.5 %all-to-all-start.1 = ((f32[16,8,128]{2,1,0:T(8,128)}), f32[16,8,128]{2,1,0:T(8,128)S(1)}, u32[]{:S(2)}, u32[]{:S(2)}) async-start(f32[16,8,128]{2,1,0:T(8,128)} %broadcast_in_dim.45), calls=%async_computation.1 | async-start | bytes 131072 | tf_op jit(solution)/shard_map/all_to_all | solution.py:38
  63.3 6.3 %all-to-all-done.1 = f32[16,8,128]{2,1,0:T(8,128)S(1)} async-done(((f32[16,8,128]{2,1,0:T(8,128)}), f32[16,8,128]{2,1,0:T(8,128)S(1)}, u32[]{:S(2)}, u32[]{:S(2)}) %all-to-all-start.1) | async-done | bytes 65568 | tf_op jit(solution)/shard_map/all_to_all | solution.py:38
  69.6 3.4 %copy-done.1 = f32[128,128,128]{2,1,0:T(8,128)S(1)} copy-done((f32[128,128,128]{2,1,0:T(8,128)S(1)}, f32[128,128,128]{2,1,0:T(8,128)}, u32[]{:S(2)}) %copy-start.1) | copy-done | bytes 8388632
  73.0 3.4 %copy-done.3 = f32[128,128,128]{2,1,0:T(8,128)S(1)} copy-done((f32[128,128,128]{2,1,0:T(8,128)S(1)}, f32[128,128,128]{2,1,0:T(8,128)}, u32[]{:S(2)}) %copy-start.3) | copy-done | bytes 8388632
  76.4 1.2 quantize.7
  77.6 1.2 quantize.6
  80.1 1.2 quantize.5
  82.2 1.2 quantize.4
  83.5 2.0 %collective-permute-start.1 = (bf16[2,4,2,128,128]{4,3,2,1,0:T(8,128)(2,1)S(1)}, bf16[2,4,2,128,128]{4,3,2,1,0:T(8,128)(2,1)S(1)}, u32[]{:S(2)}, u32[]{:S(2)}) collective-permute-start(bf16[2,4,2,128,128]{4,3,2,1,0:T(8,128)(2,1)S(1)} %get-tuple-element.45), channel_id=1, source_target_pairs={{0,1},{1,0},{2,3},{3,2},{4,5},{5,4},{6,7},{7,6},{8,9},{9,8},{10,11... | collective-permute-start | bytes 1572872 | tf_op jit(solution)/shard_map/ppermute | solution.py:30
  85.5 7.3 %collective-permute-done.13.got_ref = bf16[2,4,2,128,128]{4,3,2,1,0:T(8,128)(2,1)S(1)} collective-permute-done((bf16[2,4,2,128,128]{4,3,2,1,0:T(8,128)(2,1)S(1)}, bf16[2,4,2,128,128]{4,3,2,1,0:T(8,128)(2,1)S(1)}, u32[]{:S(2)}, u32[]{:S(2)}) %collective-permute-start.13) | collective-permute-done | bytes 524320 | tf_op jit(solution)/shard_map/ppermute | solution.py:30
  93.9 3.6 %collective-permute-start.10 = (s16[4,2,128,128]{3,2,1,0:T(8,128)(2,1)S(1)}, s16[4,2,128,128]{3,2,1,0:T(8,128)(2,1)S(1)}, u32[]{:S(2)}, u32[]{:S(2)}) collective-permute-start(s16[4,2,128,128]{3,2,1,0:T(8,128)(2,1)S(1)} %get-tuple-element.63), channel_id=1, source_target_pairs={{0,48},{1,49},{2,50},{3,51},{4,52},{5,53},{6,54},{7,55},{8,56},{9,... | collective-permute-start | bytes 786440 | tf_op jit(solution)/shard_map/ppermute | solution.py:30
  97.8 1.3 collective-permute-start.6
  100.1 1.6 collective-permute-start.15
  101.9 1.9 collective-permute-start.11
  105.0 1.8 collective-permute-start.7
  108.0 2.0 collective-permute-start.16
  110.6 1.6 collective-permute-done.7.got_ref
  112.4 1.8 collective-permute-start.4
  114.3 2.2 %collective-permute-done.8.refs_3_ = s16[2,128,128]{2,1,0:T(8,128)(2,1)S(1)} collective-permute-done((s16[2,128,128]{2,1,0:T(8,128)(2,1)S(1)}, s16[2,128,128]{2,1,0:T(8,128)(2,1)S(1)}, u32[]{:S(2)}, u32[]{:S(2)}) %collective-permute-start.8) | collective-permute-done | bytes 65568 | tf_op jit(solution)/shard_map/ppermute | solution.py:30
  116.5 1.4 collective-permute-done.4.refs_1_
  118.0 12.9 %all_to_all.20.terms_ref = s16[8,128,128]{2,1,0:T(8,128)(2,1)S(1)} all-to-all(s16[8,128,128]{2,1,0:T(8,128)(2,1)S(1)} %add_last.1), channel_id=1, replica_groups={{0,4,8,12,128,132,136,140},{1,5,9,13,129,133,137,141},{2,6,10,14,130,13..., dimensions={0} | all-to-all | bytes 524288 | tf_op jit(solution)/shard_map/all_to_all | solution.py:38
  132.0 3.4 %all-to-all-start.3 = ((bf16[8,128,128]{2,1,0:T(8,128)(2,1)}), bf16[8,128,128]{2,1,0:T(8,128)(2,1)S(1)}, u32[]{:S(2)}, u32[]{:S(2)}) async-start(bf16[8,128,128]{2,1,0:T(8,128)(2,1)} %get-tuple-element.77), calls=%async_computation.3 | async-start | bytes 524288 | tf_op jit(solution)/shard_map/all_to_all | solution.py:38
  135.5 5.9 %collective-permute-start.17 = (f32[2,32,128]{2,1,0:T(8,128)S(1)}, f32[2,32,128]{2,1,0:T(8,128)S(1)}, u32[]{:S(2)}, u32[]{:S(2)}) collective-permute-start(f32[2,32,128]{2,1,0:T(8,128)S(1)} %bitcast.52), channel_id=1, source_target_pairs={{0,128},{1,129},{2,130},{3,131},{4,132},{5,133},{6,134},{7,135},{8... | collective-permute-start | bytes 98312 | tf_op jit(solution)/shard_map/ppermute | solution.py:30
  141.4 4.4 %all-to-all-done.3 = bf16[8,128,128]{2,1,0:T(8,128)(2,1)S(1)} async-done(((bf16[8,128,128]{2,1,0:T(8,128)(2,1)}), bf16[8,128,128]{2,1,0:T(8,128)(2,1)S(1)}, u32[]{:S(2)}, u32[]{:S(2)}) %all-to-all-start.3) | async-done | bytes 262176 | tf_op jit(solution)/shard_map/all_to_all | solution.py:38
  145.8 1.4 collective-permute-start.37
  150.2 1.2 collective-permute-start.38
  152.3 1.8 collective-permute-start.32
  155.3 1.5 collective-permute-start.26
  157.8 2.0 %collective-permute-done.20 = bf16[2,2,128,128]{3,2,1,0:T(8,128)(2,1)S(1)} collective-permute-done((bf16[2,2,128,128]{3,2,1,0:T(8,128)(2,1)S(1)}, bf16[2,2,128,128]{3,2,1,0:T(8,128)(2,1)S(1)}, u32[]{:S(2)}, u32[]{:S(2)}) %collective-permute-start.20) | collective-permute-done | bytes 131104 | tf_op jit(solution)/shard_map/ppermute | solution.py:30
  159.9 1.4 collective-permute-start.21
  161.3 1.7 collective-permute-done.26
  163.1 1.7 collective-permute-start.27
  164.8 1.4 collective-permute-start.33
  166.3 2.0 %collective-permute-start.41 = (bf16[2,4,2,128,128]{4,3,2,1,0:T(8,128)(2,1)S(1)}, bf16[2,4,2,128,128]{4,3,2,1,0:T(8,128)(2,1)S(1)}, u32[]{:S(2)}, u32[]{:S(2)}) collective-permute-start(bf16[2,4,2,128,128]{4,3,2,1,0:T(8,128)(2,1)S(1)} %pad_maximum_fusion.3.refs_7_), channel_id=1, source_target_pairs={{0,48},{1,49},{2,50},{3,51},{4,52},{5,53},{6,54},{7,55},{8,56},{9,... | collective-permute-start | bytes 1572872 | tf_op jit(solution)/shard_map/ppermute | solution.py:30
  168.3 4.2 %collective-permute-done.33 = bf16[1,4,2,128,128]{4,3,2,1,0:T(8,128)(2,1)S(1)} collective-permute-done((bf16[1,4,2,128,128]{4,3,2,1,0:T(8,128)(2,1)S(1)}, bf16[1,4,2,128,128]{4,3,2,1,0:T(8,128)(2,1)S(1)}, u32[]{:S(2)}, u32[]{:S(2)}) %collective-permute-start.33) | collective-permute-done | bytes 262176 | tf_op jit(solution)/shard_map/ppermute | solution.py:30
  174.6 3.5 %collective-permute-done.41.refs_8_ = bf16[2,4,2,128,128]{4,3,2,1,0:T(8,128)(2,1)S(1)} collective-permute-done((bf16[2,4,2,128,128]{4,3,2,1,0:T(8,128)(2,1)S(1)}, bf16[2,4,2,128,128]{4,3,2,1,0:T(8,128)(2,1)S(1)}, u32[]{:S(2)}, u32[]{:S(2)}) %collective-permute-start.41) | collective-permute-done | bytes 524320 | tf_op jit(solution)/shard_map/ppermute | solution.py:30
  178.5 8.6 %collective-permute-done.35.refs_6_ = bf16[2,4,2,128,128]{4,3,2,1,0:T(8,128)(2,1)} collective-permute-done((bf16[2,4,2,128,128]{4,3,2,1,0:T(8,128)(2,1)S(1)}, bf16[2,4,2,128,128]{4,3,2,1,0:T(8,128)(2,1)}, u32[]{:S(2)}, u32[]{:S(2)}) %collective-permute-start.35) | collective-permute-done | bytes 524320 | tf_op jit(solution)/shard_map/ppermute | solution.py:30
  189.8 2.8 %collective-permute-done.23.refs_2_ = bf16[2,4,2,128,128]{4,3,2,1,0:T(8,128)(2,1)} collective-permute-done((bf16[2,4,2,128,128]{4,3,2,1,0:T(8,128)(2,1)S(1)}, bf16[2,4,2,128,128]{4,3,2,1,0:T(8,128)(2,1)}, u32[]{:S(2)}, u32[]{:S(2)}) %collective-permute-start.23) | collective-permute-done | bytes 524320 | tf_op jit(solution)/shard_map/ppermute | solution.py:30
  193.3 3.9 %assemble.2.refs_9_ = bf16[4,4,4,2,2,128,128]{6,5,4,3,2,1,0:T(8,128)(2,1)} custom-call(s32[5,8]{1,0:T(8,128)S(1)} %concatenate.77.refs_0_, bf16[2,4,2,128,128]{4,3,2,1,0:T(8,128)(2,1)S(1)} %pad_maximum_fusion.refs_1_, bf16[2,4,2,128,128]{4,3,2,1,0:T(8,128)(2,1)} %collective-permute-done.23.refs_2_, ...), custom_call_target="tpu_custom_call" | custom-call | flops 1024 | bytes 8388608 | tf_op jit(solution)/shard_map/assemble/pallas_call | solution.py:261
  197.3 4.2 %assemble.3 = bf16[4,4,4,2,2,128,128]{6,5,4,3,2,1,0:T(8,128)(2,1)} custom-call(s32[5,8]{1,0:T(8,128)S(1)} %concatenate.64.refs_0_, bf16[2,4,2,128,128]{4,3,2,1,0:T(8,128)(2,1)} %collective-permute-done.22.refs_1_, bf16[2,4,2,128,128]{4,3,2,1,0:T(8,128)(2,1)} %collective-permute-done.24.refs_2_, ...), custom_call_target="tpu_custom_call", output_to_operand_aliasing={{}: (9, {})} | custom-call | flops 1024 | bytes 8388608 | tf_op jit(solution)/shard_map/assemble/pallas_call | solution.py:261
  (134 shorter events, 23.0 us)
Async XLA Ops:
  0.7 4.9 %copy-start.10 = (s32[4]{0:T(128)S(1)}, s32[4]{0:T(128)}, u32[]{:S(2)}) copy-start(s32[4]{0:T(128)} %constant.91.clone) | copy-start | bytes 52
  0.7 4.9 %copy-start.11 = (s32[4]{0:T(128)S(1)}, s32[4]{0:T(128)}, u32[]{:S(2)}) copy-start(s32[4]{0:T(128)} %constant.89.clone) | copy-start | bytes 52
  5.5 16.3 %collective-permute-start = (bf16[4,4,4,2,1,128,128]{6,5,4,3,2,1,0:T(8,128)(2,1)}, bf16[4,4,4,2,1,128,128]{6,5,4,3,2,1,0:T(8,128)(2,1)}, u32[]{:S(2)}, u32[]{:S(2)}) collective-permute-start(bf16[4,4,4,2,1,128,128]{6,5,4,3,2,1,0:T(8,128)(2,1)} %constant_dynamic-slice_fusion), channel_id=1, source_target_pairs={{0,64},{1,65},{2,66},{3,67},{4,68},{5,69},{6,70},{7,71},{8,72},{9,... | collective-permute-start | bytes 12582920 | tf_op jit(solution)/shard_map/ppermute | solution.py:30
  38.6 16.6 %all-to-all-start = ((f32[16,8,128]{2,1,0:T(8,128)}), f32[16,8,128]{2,1,0:T(8,128)S(1)}, u32[]{:S(2)}, u32[]{:S(2)}) async-start(f32[16,8,128]{2,1,0:T(8,128)} %broadcast_in_dim.44), calls=%async_computation | async-start | bytes 131072 | tf_op jit(solution)/shard_map/all_to_all | solution.py:38
  55.8 13.8 %all-to-all-start.1 = ((f32[16,8,128]{2,1,0:T(8,128)}), f32[16,8,128]{2,1,0:T(8,128)S(1)}, u32[]{:S(2)}, u32[]{:S(2)}) async-start(f32[16,8,128]{2,1,0:T(8,128)} %broadcast_in_dim.45), calls=%async_computation.1 | async-start | bytes 131072 | tf_op jit(solution)/shard_map/all_to_all | solution.py:38
  78.9 13.9 %collective-permute-start.13 = (bf16[2,4,2,128,128]{4,3,2,1,0:T(8,128)(2,1)S(1)}, bf16[2,4,2,128,128]{4,3,2,1,0:T(8,128)(2,1)S(1)}, u32[]{:S(2)}, u32[]{:S(2)}) collective-permute-start(bf16[2,4,2,128,128]{4,3,2,1,0:T(8,128)(2,1)S(1)} %get-tuple-element.69), channel_id=1, source_target_pairs={{0,48},{1,49},{2,50},{3,51},{4,52},{5,53},{6,54},{7,55},{8,56},{9,... | collective-permute-start | bytes 1572872 | tf_op jit(solution)/shard_map/ppermute | solution.py:30
  81.3 12.3 %collective-permute-start.9 = (bf16[2,4,2,128,128]{4,3,2,1,0:T(8,128)(2,1)S(1)}, bf16[2,4,2,128,128]{4,3,2,1,0:T(8,128)(2,1)S(1)}, u32[]{:S(2)}, u32[]{:S(2)}) collective-permute-start(bf16[2,4,2,128,128]{4,3,2,1,0:T(8,128)(2,1)S(1)} %get-tuple-element.61), channel_id=1, source_target_pairs={{0,16},{1,17},{2,18},{3,19},{4,20},{5,21},{6,22},{7,23},{8,24},{9,... | collective-permute-start | bytes 1572872 | tf_op jit(solution)/shard_map/ppermute | solution.py:30
  81.4 16.1 %collective-permute-start.5 = (bf16[2,4,2,128,128]{4,3,2,1,0:T(8,128)(2,1)S(1)}, bf16[2,4,2,128,128]{4,3,2,1,0:T(8,128)(2,1)S(1)}, u32[]{:S(2)}, u32[]{:S(2)}) collective-permute-start(bf16[2,4,2,128,128]{4,3,2,1,0:T(8,128)(2,1)S(1)} %get-tuple-element.53), channel_id=1, source_target_pairs={{0,3},{1,2},{2,1},{3,0},{4,7},{5,6},{6,5},{7,4},{8,11},{9,10},{10,... | collective-permute-start | bytes 1572872 | tf_op jit(solution)/shard_map/ppermute | solution.py:30
  83.5 15.6 %collective-permute-start.1 = (bf16[2,4,2,128,128]{4,3,2,1,0:T(8,128)(2,1)S(1)}, bf16[2,4,2,128,128]{4,3,2,1,0:T(8,128)(2,1)S(1)}, u32[]{:S(2)}, u32[]{:S(2)}) collective-permute-start(bf16[2,4,2,128,128]{4,3,2,1,0:T(8,128)(2,1)S(1)} %get-tuple-element.45), channel_id=1, source_target_pairs={{0,1},{1,0},{2,3},{3,2},{4,5},{5,4},{6,7},{7,6},{8,9},{9,8},{10,11... | collective-permute-start | bytes 1572872 | tf_op jit(solution)/shard_map/ppermute | solution.py:30
  93.0 7.0 %collective-permute-start.14 = (s16[4,2,128,128]{3,2,1,0:T(8,128)(2,1)S(1)}, s16[4,2,128,128]{3,2,1,0:T(8,128)(2,1)S(1)}, u32[]{:S(2)}, u32[]{:S(2)}) collective-permute-start(s16[4,2,128,128]{3,2,1,0:T(8,128)(2,1)S(1)} %get-tuple-element.71), channel_id=1, source_target_pairs={{0,16},{1,17},{2,18},{3,19},{4,20},{5,21},{6,22},{7,23},{8,24},{9,... | collective-permute-start | bytes 786440 | tf_op jit(solution)/shard_map/ppermute | solution.py:30
  93.9 7.9 %collective-permute-start.10 = (s16[4,2,128,128]{3,2,1,0:T(8,128)(2,1)S(1)}, s16[4,2,128,128]{3,2,1,0:T(8,128)(2,1)S(1)}, u32[]{:S(2)}, u32[]{:S(2)}) collective-permute-start(s16[4,2,128,128]{3,2,1,0:T(8,128)(2,1)S(1)} %get-tuple-element.63), channel_id=1, source_target_pairs={{0,48},{1,49},{2,50},{3,51},{4,52},{5,53},{6,54},{7,55},{8,56},{9,... | collective-permute-start | bytes 786440 | tf_op jit(solution)/shard_map/ppermute | solution.py:30
  97.8 7.1 %collective-permute-start.6 = (s16[4,2,128,128]{3,2,1,0:T(8,128)(2,1)S(1)}, s16[4,2,128,128]{3,2,1,0:T(8,128)(2,1)S(1)}, u32[]{:S(2)}, u32[]{:S(2)}) collective-permute-start(s16[4,2,128,128]{3,2,1,0:T(8,128)(2,1)S(1)} %get-tuple-element.55), channel_id=1, source_target_pairs={{0,1},{1,0},{2,3},{3,2},{4,5},{5,4},{6,7},{7,6},{8,9},{9,8},{10,11... | collective-permute-start | bytes 786440 | tf_op jit(solution)/shard_map/ppermute | solution.py:30
  99.4 7.4 %collective-permute-start.2 = (s16[4,2,128,128]{3,2,1,0:T(8,128)(2,1)S(1)}, s16[4,2,128,128]{3,2,1,0:T(8,128)(2,1)S(1)}, u32[]{:S(2)}, u32[]{:S(2)}) collective-permute-start(s16[4,2,128,128]{3,2,1,0:T(8,128)(2,1)S(1)} %get-tuple-element.47), channel_id=1, source_target_pairs={{0,3},{1,2},{2,1},{3,0},{4,7},{5,6},{6,5},{7,4},{8,11},{9,10},{10,... | collective-permute-start | bytes 786440 | tf_op jit(solution)/shard_map/ppermute | solution.py:30
  100.1 7.8 %collective-permute-start.15 = (s16[2,2,128,128]{3,2,1,0:T(8,128)(2,1)S(1)}, s16[2,2,128,128]{3,2,1,0:T(8,128)(2,1)S(1)}, u32[]{:S(2)}, u32[]{:S(2)}) collective-permute-start(s16[2,2,128,128]{3,2,1,0:T(8,128)(2,1)S(1)} %get-tuple-element.73), channel_id=1, source_target_pairs={{0,3},{1,2},{2,1},{3,0},{4,7},{5,6},{6,5},{7,4},{8,11},{9,10},{10,... | collective-permute-start | bytes 393224 | tf_op jit(solution)/shard_map/ppermute | solution.py:30
  101.9 8.0 %collective-permute-start.11 = (s16[2,2,128,128]{3,2,1,0:T(8,128)(2,1)S(1)}, s16[2,2,128,128]{3,2,1,0:T(8,128)(2,1)S(1)}, u32[]{:S(2)}, u32[]{:S(2)}) collective-permute-start(s16[2,2,128,128]{3,2,1,0:T(8,128)(2,1)S(1)} %get-tuple-element.65), channel_id=1, source_target_pairs={{0,1},{1,0},{2,3},{3,2},{4,5},{5,4},{6,7},{7,6},{8,9},{9,8},{10,11... | collective-permute-start | bytes 393224 | tf_op jit(solution)/shard_map/ppermute | solution.py:30
  105.0 7.1 %collective-permute-start.7 = (s16[2,2,128,128]{3,2,1,0:T(8,128)(2,1)S(1)}, s16[2,2,128,128]{3,2,1,0:T(8,128)(2,1)S(1)}, u32[]{:S(2)}, u32[]{:S(2)}) collective-permute-start(s16[2,2,128,128]{3,2,1,0:T(8,128)(2,1)S(1)} %get-tuple-element.57), channel_id=1, source_target_pairs={{0,48},{1,49},{2,50},{3,51},{4,52},{5,53},{6,54},{7,55},{8,56},{9,... | collective-permute-start | bytes 393224 | tf_op jit(solution)/shard_map/ppermute | solution.py:30
  106.9 5.4 %collective-permute-start.3 = (s16[2,2,128,128]{3,2,1,0:T(8,128)(2,1)S(1)}, s16[2,2,128,128]{3,2,1,0:T(8,128)(2,1)S(1)}, u32[]{:S(2)}, u32[]{:S(2)}) collective-permute-start(s16[2,2,128,128]{3,2,1,0:T(8,128)(2,1)S(1)} %get-tuple-element.49), channel_id=1, source_target_pairs={{0,16},{1,17},{2,18},{3,19},{4,20},{5,21},{6,22},{7,23},{8,24},{9,... | collective-permute-start | bytes 393224 | tf_op jit(solution)/shard_map/ppermute | solution.py:30
  108.0 6.2 %collective-permute-start.16 = (s16[2,128,128]{2,1,0:T(8,128)(2,1)S(1)}, s16[2,128,128]{2,1,0:T(8,128)(2,1)S(1)}, u32[]{:S(2)}, u32[]{:S(2)}) collective-permute-start(s16[2,128,128]{2,1,0:T(8,128)(2,1)S(1)} %get-tuple-element.75), channel_id=1, source_target_pairs={{0,1},{1,0},{2,3},{3,2},{4,5},{5,4},{6,7},{7,6},{8,9},{9,8},{10,11... | collective-permute-start | bytes 196616 | tf_op jit(solution)/shard_map/ppermute | solution.py:30
  110.0 4.4 %collective-permute-start.12 = (s16[2,128,128]{2,1,0:T(8,128)(2,1)S(1)}, s16[2,128,128]{2,1,0:T(8,128)(2,1)S(1)}, u32[]{:S(2)}, u32[]{:S(2)}) collective-permute-start(s16[2,128,128]{2,1,0:T(8,128)(2,1)S(1)} %get-tuple-element.67), channel_id=1, source_target_pairs={{0,3},{1,2},{2,1},{3,0},{4,7},{5,6},{6,5},{7,4},{8,11},{9,10},{10,... | collective-permute-start | bytes 196616 | tf_op jit(solution)/shard_map/ppermute | solution.py:30
  112.1 4.4 %collective-permute-start.8 = (s16[2,128,128]{2,1,0:T(8,128)(2,1)S(1)}, s16[2,128,128]{2,1,0:T(8,128)(2,1)S(1)}, u32[]{:S(2)}, u32[]{:S(2)}) collective-permute-start(s16[2,128,128]{2,1,0:T(8,128)(2,1)S(1)} %get-tuple-element.59), channel_id=1, source_target_pairs={{0,16},{1,17},{2,18},{3,19},{4,20},{5,21},{6,22},{7,23},{8,24},{9,... | collective-permute-start | bytes 196616 | tf_op jit(solution)/shard_map/ppermute | solution.py:30
  112.4 5.6 %collective-permute-start.4 = (s16[2,128,128]{2,1,0:T(8,128)(2,1)S(1)}, s16[2,128,128]{2,1,0:T(8,128)(2,1)S(1)}, u32[]{:S(2)}, u32[]{:S(2)}) collective-permute-start(s16[2,128,128]{2,1,0:T(8,128)(2,1)S(1)} %get-tuple-element.51), channel_id=1, source_target_pairs={{0,48},{1,49},{2,50},{3,51},{4,52},{5,53},{6,54},{7,55},{8,56},{9,... | collective-permute-start | bytes 196616 | tf_op jit(solution)/shard_map/ppermute | solution.py:30
  132.0 13.8 %all-to-all-start.3 = ((bf16[8,128,128]{2,1,0:T(8,128)(2,1)}), bf16[8,128,128]{2,1,0:T(8,128)(2,1)S(1)}, u32[]{:S(2)}, u32[]{:S(2)}) async-start(bf16[8,128,128]{2,1,0:T(8,128)(2,1)} %get-tuple-element.77), calls=%async_computation.3 | async-start | bytes 524288 | tf_op jit(solution)/shard_map/all_to_all | solution.py:38
  135.5 11.8 %collective-permute-start.17 = (f32[2,32,128]{2,1,0:T(8,128)S(1)}, f32[2,32,128]{2,1,0:T(8,128)S(1)}, u32[]{:S(2)}, u32[]{:S(2)}) collective-permute-start(f32[2,32,128]{2,1,0:T(8,128)S(1)} %bitcast.52), channel_id=1, source_target_pairs={{0,128},{1,129},{2,130},{3,131},{4,132},{5,133},{6,134},{7,135},{8... | collective-permute-start | bytes 98312 | tf_op jit(solution)/shard_map/ppermute | solution.py:30
  145.8 4.4 %collective-permute-start.37 = (bf16[1,2,128,128]{3,2,1,0:T(8,128)(2,1)S(1)}, bf16[1,2,128,128]{3,2,1,0:T(8,128)(2,1)S(1)}, u32[]{:S(2)}, u32[]{:S(2)}) collective-permute-start(bf16[1,2,128,128]{3,2,1,0:T(8,128)(2,1)S(1)} %get-tuple-element.78), channel_id=1, source_target_pairs={{0,1},{1,0},{2,3},{3,2},{4,5},{5,4},{6,7},{7,6},{8,9},{9,8},{10,11... | collective-permute-start | bytes 196616 | tf_op jit(solution)/shard_map/ppermute | solution.py:30
  147.2 5.0 %collective-permute-start.31 = (bf16[1,2,128,128]{3,2,1,0:T(8,128)(2,1)S(1)}, bf16[1,2,128,128]{3,2,1,0:T(8,128)(2,1)S(1)}, u32[]{:S(2)}, u32[]{:S(2)}) collective-permute-start(bf16[1,2,128,128]{3,2,1,0:T(8,128)(2,1)S(1)} %get-tuple-element.79), channel_id=1, source_target_pairs={{0,3},{1,2},{2,1},{3,0},{4,7},{5,6},{6,5},{7,4},{8,11},{9,10},{10,... | collective-permute-start | bytes 196616 | tf_op jit(solution)/shard_map/ppermute | solution.py:30
  148.3 7.0 %collective-permute-start.25 = (bf16[1,2,128,128]{3,2,1,0:T(8,128)(2,1)S(1)}, bf16[1,2,128,128]{3,2,1,0:T(8,128)(2,1)S(1)}, u32[]{:S(2)}, u32[]{:S(2)}) collective-permute-start(bf16[1,2,128,128]{3,2,1,0:T(8,128)(2,1)S(1)} %get-tuple-element.80), channel_id=1, source_target_pairs={{0,16},{1,17},{2,18},{3,19},{4,20},{5,21},{6,22},{7,23},{8,24},{9,... | collective-permute-start | bytes 196616 | tf_op jit(solution)/shard_map/ppermute | solution.py:30
  149.1 5.7 %collective-permute-start.19 = (bf16[1,2,128,128]{3,2,1,0:T(8,128)(2,1)S(1)}, bf16[1,2,128,128]{3,2,1,0:T(8,128)(2,1)S(1)}, u32[]{:S(2)}, u32[]{:S(2)}) collective-permute-start(bf16[1,2,128,128]{3,2,1,0:T(8,128)(2,1)S(1)} %get-tuple-element.81), channel_id=1, source_target_pairs={{0,48},{1,49},{2,50},{3,51},{4,52},{5,53},{6,54},{7,55},{8,56},{9,... | collective-permute-start | bytes 196616 | tf_op jit(solution)/shard_map/ppermute | solution.py:30
  150.2 6.7 %collective-permute-start.38 = (bf16[2,2,128,128]{3,2,1,0:T(8,128)(2,1)S(1)}, bf16[2,2,128,128]{3,2,1,0:T(8,128)(2,1)S(1)}, u32[]{:S(2)}, u32[]{:S(2)}) collective-permute-start(bf16[2,2,128,128]{3,2,1,0:T(8,128)(2,1)S(1)} %pad_maximum_fusion.7), channel_id=1, source_target_pairs={{0,3},{1,2},{2,1},{3,0},{4,7},{5,6},{6,5},{7,4},{8,11},{9,10},{10,... | collective-permute-start | bytes 393224 | tf_op jit(solution)/shard_map/ppermute | solution.py:30
  152.3 12.5 %collective-permute-start.32 = (bf16[2,2,128,128]{3,2,1,0:T(8,128)(2,1)S(1)}, bf16[2,2,128,128]{3,2,1,0:T(8,128)(2,1)S(1)}, u32[]{:S(2)}, u32[]{:S(2)}) collective-permute-start(bf16[2,2,128,128]{3,2,1,0:T(8,128)(2,1)S(1)} %pad_maximum_fusion.6), channel_id=1, source_target_pairs={{0,1},{1,0},{2,3},{3,2},{4,5},{5,4},{6,7},{7,6},{8,9},{9,8},{10,11... | collective-permute-start | bytes 393224 | tf_op jit(solution)/shard_map/ppermute | solution.py:30
  154.8 5.1 %collective-permute-start.20 = (bf16[2,2,128,128]{3,2,1,0:T(8,128)(2,1)S(1)}, bf16[2,2,128,128]{3,2,1,0:T(8,128)(2,1)S(1)}, u32[]{:S(2)}, u32[]{:S(2)}) collective-permute-start(bf16[2,2,128,128]{3,2,1,0:T(8,128)(2,1)S(1)} %pad_maximum_fusion.4), channel_id=1, source_target_pairs={{0,16},{1,17},{2,18},{3,19},{4,20},{5,21},{6,22},{7,23},{8,24},{9,... | collective-permute-start | bytes 393224 | tf_op jit(solution)/shard_map/ppermute | solution.py:30
  155.3 7.7 %collective-permute-start.26 = (bf16[2,2,128,128]{3,2,1,0:T(8,128)(2,1)S(1)}, bf16[2,2,128,128]{3,2,1,0:T(8,128)(2,1)S(1)}, u32[]{:S(2)}, u32[]{:S(2)}) collective-permute-start(bf16[2,2,128,128]{3,2,1,0:T(8,128)(2,1)S(1)} %pad_maximum_fusion.5), channel_id=1, source_target_pairs={{0,48},{1,49},{2,50},{3,51},{4,52},{5,53},{6,54},{7,55},{8,56},{9,... | collective-permute-start | bytes 393224 | tf_op jit(solution)/shard_map/ppermute | solution.py:30
  156.9 9.3 %collective-permute-start.39 = (bf16[1,4,2,128,128]{4,3,2,1,0:T(8,128)(2,1)S(1)}, bf16[1,4,2,128,128]{4,3,2,1,0:T(8,128)(2,1)S(1)}, u32[]{:S(2)}, u32[]{:S(2)}) collective-permute-start(bf16[1,4,2,128,128]{4,3,2,1,0:T(8,128)(2,1)S(1)} %maximum_bitcast_fusion.3), channel_id=1, source_target_pairs={{0,16},{1,17},{2,18},{3,19},{4,20},{5,21},{6,22},{7,23},{8,24},{9,... | collective-permute-start | bytes 786440 | tf_op jit(solution)/shard_map/ppermute | solution.py:30
  159.9 12.7 %collective-permute-start.21 = (bf16[1,4,2,128,128]{4,3,2,1,0:T(8,128)(2,1)S(1)}, bf16[1,4,2,128,128]{4,3,2,1,0:T(8,128)(2,1)S(1)}, u32[]{:S(2)}, u32[]{:S(2)}) collective-permute-start(bf16[1,4,2,128,128]{4,3,2,1,0:T(8,128)(2,1)S(1)} %maximum_bitcast_fusion), channel_id=1, source_target_pairs={{0,3},{1,2},{2,1},{3,0},{4,7},{5,6},{6,5},{7,4},{8,11},{9,10},{10,... | collective-permute-start | bytes 786440 | tf_op jit(solution)/shard_map/ppermute | solution.py:30
  163.1 9.7 %collective-permute-start.27 = (bf16[1,4,2,128,128]{4,3,2,1,0:T(8,128)(2,1)S(1)}, bf16[1,4,2,128,128]{4,3,2,1,0:T(8,128)(2,1)S(1)}, u32[]{:S(2)}, u32[]{:S(2)}) collective-permute-start(bf16[1,4,2,128,128]{4,3,2,1,0:T(8,128)(2,1)S(1)} %maximum_bitcast_fusion.1), channel_id=1, source_target_pairs={{0,1},{1,0},{2,3},{3,2},{4,5},{5,4},{6,7},{7,6},{8,9},{9,8},{10,11... | collective-permute-start | bytes 786440 | tf_op jit(solution)/shard_map/ppermute | solution.py:30
  164.8 7.7 %collective-permute-start.33 = (bf16[1,4,2,128,128]{4,3,2,1,0:T(8,128)(2,1)S(1)}, bf16[1,4,2,128,128]{4,3,2,1,0:T(8,128)(2,1)S(1)}, u32[]{:S(2)}, u32[]{:S(2)}) collective-permute-start(bf16[1,4,2,128,128]{4,3,2,1,0:T(8,128)(2,1)S(1)} %maximum_bitcast_fusion.2), channel_id=1, source_target_pairs={{0,48},{1,49},{2,50},{3,51},{4,52},{5,53},{6,54},{7,55},{8,56},{9,... | collective-permute-start | bytes 786440 | tf_op jit(solution)/shard_map/ppermute | solution.py:30
  166.3 11.9 %collective-permute-start.41 = (bf16[2,4,2,128,128]{4,3,2,1,0:T(8,128)(2,1)S(1)}, bf16[2,4,2,128,128]{4,3,2,1,0:T(8,128)(2,1)S(1)}, u32[]{:S(2)}, u32[]{:S(2)}) collective-permute-start(bf16[2,4,2,128,128]{4,3,2,1,0:T(8,128)(2,1)S(1)} %pad_maximum_fusion.3.refs_7_), channel_id=1, source_target_pairs={{0,48},{1,49},{2,50},{3,51},{4,52},{5,53},{6,54},{7,55},{8,56},{9,... | collective-permute-start | bytes 1572872 | tf_op jit(solution)/shard_map/ppermute | solution.py:30
  168.3 9.8 %collective-permute-start.40 = (bf16[2,4,2,128,128]{4,3,2,1,0:T(8,128)(2,1)S(1)}, bf16[2,4,2,128,128]{4,3,2,1,0:T(8,128)(2,1)S(1)}, u32[]{:S(2)}, u32[]{:S(2)}) collective-permute-start(bf16[2,4,2,128,128]{4,3,2,1,0:T(8,128)(2,1)S(1)} %pad_maximum_fusion.3.refs_7_), channel_id=1, source_target_pairs={{0,64},{1,65},{2,66},{3,67},{4,68},{5,69},{6,70},{7,71},{8,72},{9,... | collective-permute-start | bytes 1572872 | tf_op jit(solution)/shard_map/ppermute | solution.py:30
  172.5 1.2 collective-permute-start.18
  172.6 14.5 %collective-permute-start.35 = (bf16[2,4,2,128,128]{4,3,2,1,0:T(8,128)(2,1)S(1)}, bf16[2,4,2,128,128]{4,3,2,1,0:T(8,128)(2,1)}, u32[]{:S(2)}, u32[]{:S(2)}) collective-permute-start(bf16[2,4,2,128,128]{4,3,2,1,0:T(8,128)(2,1)S(1)} %pad_maximum_fusion.2.refs_5_), channel_id=1, source_target_pairs={{0,16},{1,17},{2,18},{3,19},{4,20},{5,21},{6,22},{7,23},{8,24},{9,... | collective-permute-start | bytes 1572872 | tf_op jit(solution)/shard_map/ppermute | solution.py:30
  172.7 14.4 %collective-permute-start.34 = (bf16[2,4,2,128,128]{4,3,2,1,0:T(8,128)(2,1)S(1)}, bf16[2,4,2,128,128]{4,3,2,1,0:T(8,128)(2,1)S(1)}, u32[]{:S(2)}, u32[]{:S(2)}) collective-permute-start(bf16[2,4,2,128,128]{4,3,2,1,0:T(8,128)(2,1)S(1)} %pad_maximum_fusion.2.refs_5_), channel_id=1, source_target_pairs={{0,64},{1,65},{2,66},{3,67},{4,68},{5,69},{6,70},{7,71},{8,72},{9,... | collective-permute-start | bytes 1572872 | tf_op jit(solution)/shard_map/ppermute | solution.py:30
  173.7 14.7 %collective-permute-start.29 = (bf16[2,4,2,128,128]{4,3,2,1,0:T(8,128)(2,1)S(1)}, bf16[2,4,2,128,128]{4,3,2,1,0:T(8,128)(2,1)}, u32[]{:S(2)}, u32[]{:S(2)}) collective-permute-start(bf16[2,4,2,128,128]{4,3,2,1,0:T(8,128)(2,1)S(1)} %pad_maximum_fusion.1.refs_3_), channel_id=1, source_target_pairs={{0,3},{1,2},{2,1},{3,0},{4,7},{5,6},{6,5},{7,4},{8,11},{9,10},{10,... | collective-permute-start | bytes 1572872 | tf_op jit(solution)/shard_map/ppermute | solution.py:30
  178.1 10.3 %collective-permute-start.28 = (bf16[2,4,2,128,128]{4,3,2,1,0:T(8,128)(2,1)S(1)}, bf16[2,4,2,128,128]{4,3,2,1,0:T(8,128)(2,1)S(1)}, u32[]{:S(2)}, u32[]{:S(2)}) collective-permute-start(bf16[2,4,2,128,128]{4,3,2,1,0:T(8,128)(2,1)S(1)} %pad_maximum_fusion.1.refs_3_), channel_id=1, source_target_pairs={{0,64},{1,65},{2,66},{3,67},{4,68},{5,69},{6,70},{7,71},{8,72},{9,... | collective-permute-start | bytes 1572872 | tf_op jit(solution)/shard_map/ppermute | solution.py:30
  178.1 14.4 %collective-permute-start.23 = (bf16[2,4,2,128,128]{4,3,2,1,0:T(8,128)(2,1)S(1)}, bf16[2,4,2,128,128]{4,3,2,1,0:T(8,128)(2,1)}, u32[]{:S(2)}, u32[]{:S(2)}) collective-permute-start(bf16[2,4,2,128,128]{4,3,2,1,0:T(8,128)(2,1)S(1)} %pad_maximum_fusion.refs_1_), channel_id=1, source_target_pairs={{0,1},{1,0},{2,3},{3,2},{4,5},{5,4},{6,7},{7,6},{8,9},{9,8},{10,11... | collective-permute-start | bytes 1572872 | tf_op jit(solution)/shard_map/ppermute | solution.py:30
  187.1 10.1 %collective-permute-start.22 = (bf16[2,4,2,128,128]{4,3,2,1,0:T(8,128)(2,1)S(1)}, bf16[2,4,2,128,128]{4,3,2,1,0:T(8,128)(2,1)}, u32[]{:S(2)}, u32[]{:S(2)}) collective-permute-start(bf16[2,4,2,128,128]{4,3,2,1,0:T(8,128)(2,1)S(1)} %pad_maximum_fusion.refs_1_), channel_id=1, source_target_pairs={{0,64},{1,65},{2,66},{3,67},{4,68},{5,69},{6,70},{7,71},{8,72},{9,... | collective-permute-start | bytes 1572872 | tf_op jit(solution)/shard_map/ppermute | solution.py:30
  187.9 9.3 %collective-permute-start.42 = (bf16[2,4,2,128,128]{4,3,2,1,0:T(8,128)(2,1)S(1)}, bf16[2,4,2,128,128]{4,3,2,1,0:T(8,128)(2,1)}, u32[]{:S(2)}, u32[]{:S(2)}) collective-permute-start(bf16[2,4,2,128,128]{4,3,2,1,0:T(8,128)(2,1)S(1)} %collective-permute-done.41.refs_8_), channel_id=1, source_target_pairs={{0,64},{1,65},{2,66},{3,67},{4,68},{5,69},{6,70},{7,71},{8,72},{9,... | collective-permute-start | bytes 1572872 | tf_op jit(solution)/shard_map/ppermute | solution.py:30
  188.4 8.8 %collective-permute-start.36 = (bf16[2,4,2,128,128]{4,3,2,1,0:T(8,128)(2,1)}, bf16[2,4,2,128,128]{4,3,2,1,0:T(8,128)(2,1)}, u32[]{:S(2)}, u32[]{:S(2)}) collective-permute-start(bf16[2,4,2,128,128]{4,3,2,1,0:T(8,128)(2,1)} %collective-permute-done.35.refs_6_), channel_id=1, source_target_pairs={{0,64},{1,65},{2,66},{3,67},{4,68},{5,69},{6,70},{7,71},{8,72},{9,... | collective-permute-start | bytes 1572872 | tf_op jit(solution)/shard_map/ppermute | solution.py:30
  189.3 8.0 %collective-permute-start.30 = (bf16[2,4,2,128,128]{4,3,2,1,0:T(8,128)(2,1)}, bf16[2,4,2,128,128]{4,3,2,1,0:T(8,128)(2,1)}, u32[]{:S(2)}, u32[]{:S(2)}) collective-permute-start(bf16[2,4,2,128,128]{4,3,2,1,0:T(8,128)(2,1)} %collective-permute-done.29.refs_4_), channel_id=1, source_target_pairs={{0,64},{1,65},{2,66},{3,67},{4,68},{5,69},{6,70},{7,71},{8,72},{9,... | collective-permute-start | bytes 1572872 | tf_op jit(solution)/shard_map/ppermute | solution.py:30
  192.6 4.7 %collective-permute-start.24 = (bf16[2,4,2,128,128]{4,3,2,1,0:T(8,128)(2,1)}, bf16[2,4,2,128,128]{4,3,2,1,0:T(8,128)(2,1)}, u32[]{:S(2)}, u32[]{:S(2)}) collective-permute-start(bf16[2,4,2,128,128]{4,3,2,1,0:T(8,128)(2,1)} %collective-permute-done.23.refs_2_), channel_id=1, source_target_pairs={{0,64},{1,65},{2,66},{3,67},{4,68},{5,69},{6,70},{7,71},{8,72},{9,... | collective-permute-start | bytes 1572872 | tf_op jit(solution)/shard_map/ppermute | solution.py:30
  (12 other events, 42.6 us)
